TPU v7x, 32 devices: a whole 2x2x4 slice. The times are simulated.
32 devices in a mesh: edge: 8 (over z, y), node: 4 (over x, core).
Axes of the slice: x: 2, y: 2, z: 4, core: 2. Of those that a mesh axis runs over, the one named last changes fastest.
Arguments:
- residual: float32 [64, 32768], P(None, ('edge', 'node')), may hold values from -6 to 6
- tangent: float32 [3, 64, 32768], P(None, None, ('edge', 'node')), may hold values from -4 to 4
- jacobi: float32 [64, 32768], P(None, ('edge', 'node')), may hold values from 0.2 to 1
- ends: int32 [2, 64, 32768], P(None, None, ('edge', 'node')), may hold values from 0 to 31, as said below
- target: int32 [32768, 1], P(('edge', 'node')), may hold values from 0 to 31; in each aligned block of 1024 rows (0 to 1023, 1024 to 2047, ...) at most 64 rows name the same one
- node_block: int32 [32768], P(('edge', 'node')), may hold values from 0 to 1023
- sigma: float32 [128, 32, 256], P(('edge', 'node')), may hold values from 0.25 to 8
Outputs:
- correction: float32 [64, 32768], P(None, ('edge', 'node'))
Inputs may be any that keep to these rules, and one draw needn't show every extreme that they name: `ends`: the head and tail of an edge differ. `target`: among the 1024 rows of one device no device is named more than 64 times, and one is named exactly 64 times.
All inputs are finite; a program needn't handle non-finite values.
Results may differ from a plain program's by a relative error of at most 0.000086.
Values sent between devices are 32-bit elements; how exact they have to be, the bound alone decides.
A program may use at most 64 MiB of HBM per device.

v0:
```python
import math

import jax
import jax.numpy as jnp
from jax import lax
from jax.sharding import PartitionSpec as P

BLOCK_EDGES = 64
NODE_BLOCK = 32


mass_scale = (1.0, 1.0, 1.0, 0.5)


def with_halo(cells, sides, width):
    for axis, dim in sides:
        count = lax.axis_size(axis)
        head = lax.slice_in_dim(cells, 0, width, axis=dim)
        tail = lax.slice_in_dim(cells, cells.shape[dim] - width, cells.shape[dim], axis=dim)
        cells = jnp.concatenate(
            [
                lax.ppermute(tail, axis, [(i, (i + 1) % count) for i in range(count)]),
                cells,
                lax.ppermute(head, axis, [((i + 1) % count, i) for i in range(count)]),
            ],
            axis=dim,
        )
    return cells


def chebyshev_terms():
    scale = jnp.array(mass_scale, jnp.float32).reshape(4, 1, 1, 1)
    upper = 12.0 + 8.0 * scale
    lower = upper / 8.0
    centre = (upper + lower) / 2.0
    radius = (upper - lower) / 2.0
    ratio = centre / radius
    first = 1.0 / ratio
    second = 1.0 / (2.0 * ratio - first)
    return (scale, centre, second * first, 2.0 * second / radius)


def stiffness(padded, diag):
    centre = padded[:, 1:-1]
    beside_all = padded[:, :-2] + padded[:, 2:]
    inner = jnp.pad(centre, ((0, 0), (0, 0), (1, 1), (1, 1)))
    beside_all = beside_all + inner[:, :, :-2, 1:-1] + inner[:, :, 2:, 1:-1]
    beside_all = beside_all + inner[:, :, 1:-1, :-2] + inner[:, :, 1:-1, 2:]
    return diag * centre - beside_all


def hot_pair(ends_part):
    node_ids = jnp.arange(NODE_BLOCK, dtype=jnp.int32)[None, :, None]
    head_hot = (ends_part[1][:, None, :] == node_ids).astype(jnp.float32)
    tail_hot = (ends_part[0][:, None, :] == node_ids).astype(jnp.float32)
    return (head_hot, tail_hot)


def group_last(array, group_size):
    leading = array.shape[:-1]
    groups = array.shape[-1] // group_size
    return jnp.moveaxis(array.reshape(leading + (groups, group_size)), -2, 0)


def block_terms(residual, tangent, ends, group_size):
    width = 4 * NODE_BLOCK
    highest = lax.Precision.HIGHEST

    def block_one_group(pieces):
        resid_part, tangent_part, ends_part = pieces
        head_hot, tail_hot = hot_pair(ends_part)
        vector_part = 0.5 * tangent_part * resid_part[None]
        vector_out = jnp.einsum("ceb,enb->bcn", vector_part, head_hot + tail_hot, precision=highest)
        scalar_out = jnp.einsum("eb,enb->bn", resid_part, head_hot - tail_hot, precision=highest)
        return jnp.concatenate([vector_out, scalar_out[:, None]], axis=1).reshape(group_size, width)

    grouped = lax.map(
        block_one_group,
        (
            group_last(residual, group_size),
            group_last(tangent, group_size),
            group_last(ends, group_size),
        ),
    )
    return grouped.reshape(-1, width)


def lift_values(values, tangent, ends, group_size):
    highest = lax.Precision.HIGHEST
    groups = values.shape[0] // group_size
    value_groups = values.reshape(groups, group_size, 4, NODE_BLOCK)

    def lift_one_group(pieces):
        value_part, tangent_part, ends_part = pieces
        head_hot, tail_hot = hot_pair(ends_part)
        vector_sum = jnp.einsum(
            "bcn,enb->ceb", value_part[:, :3], head_hot + tail_hot, precision=highest
        )
        scalar_diff = jnp.einsum(
            "bn,enb->eb", value_part[:, 3], head_hot - tail_hot, precision=highest
        )
        return 0.5 * jnp.sum(tangent_part * vector_sum, axis=0) + scalar_diff

    lifted = lax.map(
        lift_one_group,
        (value_groups, group_last(tangent, group_size), group_last(ends, group_size)),
    )
    return jnp.moveaxis(lifted, 0, 1).reshape(BLOCK_EDGES, -1)


def per_device(residual, tangent, jacobi, ends, target, node_block, sigma):
    devices = lax.axis_size(("edge", "node"))
    blocks_mine = residual.shape[1]
    group_size = math.gcd(blocks_mine, 512)
    capacity = max(2, 2 * blocks_mine // devices)
    slots_all = devices * capacity
    slices, rows_radial, rows_axial = sigma.shape
    nodal_blocks = slices * rows_radial * rows_axial // NODE_BLOCK
    width = 4 * NODE_BLOCK
    target_dev = target[:, 0]
    matches = (target_dev[:, None] == jnp.arange(devices, dtype=jnp.int32)[None, :]).astype(
        jnp.int32
    )
    ranking = jnp.cumsum(matches, axis=0)
    slot_rank = jnp.sum(ranking * matches, axis=1) - 1
    position = target_dev * capacity + slot_rank
    labels = jnp.full((slots_all,), -1, jnp.int32).at[position].set(node_block)
    block_rows = block_terms(residual, tangent, ends, group_size)
    partials = jnp.zeros((slots_all, width), jnp.float32).at[position].set(block_rows)
    got_terms, got_labels = (
        lax.all_to_all(
            partials.reshape(devices, capacity, width),
            ("edge", "node"),
            split_axis=0,
            concat_axis=0,
            tiled=True,
        ),
        lax.all_to_all(
            labels.reshape(devices, capacity),
            ("edge", "node"),
            split_axis=0,
            concat_axis=0,
            tiled=True,
        ),
    )
    got_terms = got_terms.reshape(slots_all, width)
    got_labels = got_labels.reshape(slots_all)
    safe_labels = jnp.where(got_labels < 0, nodal_blocks, got_labels)
    summed = jax.ops.segment_sum(got_terms, safe_labels, num_segments=nodal_blocks + 1)[
        :nodal_blocks
    ]
    source = summed.reshape(slices, rows_radial * rows_axial // NODE_BLOCK, 4, NODE_BLOCK)
    source = source.transpose(2, 0, 1, 3).reshape(4, slices, rows_radial, rows_axial)
    scale, centre, coef_one, coef_two = chebyshev_terms()
    diag = 6.0 + scale * sigma[None]

    def apply(field):
        padded = with_halo(field, ((("edge", "node"), 1),), 1)
        return stiffness(padded, diag)

    step_one = source / centre
    rest = source - apply(step_one)
    step_two = coef_one * step_one + coef_two * rest
    solution = step_one + step_two
    rest = source - apply(solution)
    step_one = rest / centre
    rest = rest - apply(step_one)
    step_two = coef_one * step_one + coef_two * rest
    solution = solution + step_one + step_two
    sol_blocks = solution.reshape(4, slices, rows_radial * rows_axial // NODE_BLOCK, NODE_BLOCK)
    sol_blocks = sol_blocks.transpose(1, 2, 0, 3).reshape(nodal_blocks, width)
    outgoing = sol_blocks[jnp.clip(got_labels, 0, nodal_blocks - 1)]
    returned = lax.all_to_all(
        outgoing.reshape(devices, capacity, width),
        ("edge", "node"),
        split_axis=0,
        concat_axis=0,
        tiled=True,
    )
    mine = returned.reshape(slots_all, width)[position]
    lifted = lift_values(mine, tangent, ends, group_size)
    return jacobi * residual + lifted


def solution(mesh):
    in_specs = (
        P(None, ("edge", "node")),
        P(None, None, ("edge", "node")),
        P(None, ("edge", "node")),
        P(None, None, ("edge", "node")),
        P(("edge", "node"), None),
        P(("edge", "node")),
        P(("edge", "node"), None, None),
    )
    out_specs = P(None, ("edge", "node"))
    return jax.shard_map(
        per_device, mesh=mesh, in_specs=in_specs, out_specs=out_specs, check_vma=False
    )
```

profile of v0, /device:TPU:0, one launch (start us, length us, event | category | flops | bytes accessed | tf_op | source)
XLA Modules:
  0.0 286.2 jit_solution(1708787834374360602)
XLA Ops:
  0.8 9.0 %reduce-window.6 = s32[32,8,128]{2,1,0:T(8,128)S(1)} reduce-window(s32[32,8,128]{2,1,0:T(8,128)S(1)} %fusion.52, s32[]{:T(128)} %constant.26.clone.1), window={size=1x1x128 pad=0_0x0_0x127_0}, to_apply=%region_0.0 | reduce-window | flops 4161536 | bytes 262148 | tf_op jit(solution)/shard_map/reduce-window
  11.7 4.5 %scatter_custom_fusion = s32[2048]{0:T(1024)S(1)} fusion(s32[1024]{0:T(1024)S(1)} %bitcast.131, s32[1024]{0:T(1024)} %param.17, s32[]{:T(128)} %constant.36.clone.1), kind=kCustom, calls=%fused_computation.108 | custom fusion | bytes 8704 | tf_op jit(solution)/shard_map/scatter | solution.py:127
  16.9 7.3 %all-to-all-start = ((s32[32,1,64]{2,1,0:T(1,128)}), s32[32,1,64]{2,1,0:T(1,128)S(1)}, u32[]{:S(2)}, u32[]{:S(2)}) async-start(s32[32,1,64]{2,1,0:T(1,128)} %all_to_all.12), calls=%async_computation | async-start | bytes 32768 | tf_op jit(solution)/shard_map/all_to_all | solution.py:138
  28.7 81.6 %while.20 = (s32[]{:T(128)}, f32[2,512,128]{2,1,0:T(8,128)}, f32[2,3,64,512]{2,1,3,0:T(4,128)}, f32[2,64,512]{1,2,0:T(8,128)}, s32[2,2,64,512]{2,3,1,0:T(8,128)S(1)}, /*index=5*/s32[]{:T(128)}, s32[]{:T(128)}, s32[]{}) while((s32[]{:T(128)}, f32[2,512,128]{2,1,0:T(8,128)}, f32[2,3,64,512]{2,1,3,0:T(4,128)}, f32[2,64,512]{1,2,0:T(8,128)}, ...), condition=%wide.region_5.6_spmd, body=%wide.region_4.5_spmd.sunk | while | flops 61014016 | bytes 9306793 | solution.py:77
  47.1 15.5 %fusion.68 = f32[512,3,32]{2,1,0:T(4,128)S(1)} fusion(s32[64,512]{0,1:T(8,128)S(1)} %get-tuple-element.191, s32[64,512]{0,1:T(8,128)S(1)} %get-tuple-element.192, f32[2,3,64,512]{2,1,3,0:T(4,128)} %get-tuple-element.219, s32[]{:T(128)} %get-tuple-element.209, f32[64,512]{0,1:T(8,128)S(1)} %get-tuple-element.193), kind=kOutput, calls=%fused_computation.7.clone.1 | convolution fusion | flops 43089920 | bytes 1638912 | tf_op jit(solution)/shard_map/while/body/eval_jaxpr/ceb,enb->bcn/dot_general | solution.py:73
  62.8 14.0 %fusion.67 = f32[512,1,32]{2,1,0:T(1,128)S(1)} fusion(f32[64,512,1]{0,2,1:T(1,128)S(1)} %bitcast.118, s32[64,512]{0,1:T(8,128)S(1)} %get-tuple-element.191, s32[64,512]{0,1:T(8,128)S(1)} %get-tuple-element.192), kind=kOutput, calls=%fused_computation.8.clone.1 | convolution fusion | flops 17825792 | bytes 458752 | tf_op jit(solution)/shard_map/while/body/eval_jaxpr/eb,enb->bn/dot_general | solution.py:74
  79.0 15.5 %fusion.68 = f32[512,3,32]{2,1,0:T(4,128)S(1)} fusion(s32[64,512]{0,1:T(8,128)S(1)} %get-tuple-element.191, s32[64,512]{0,1:T(8,128)S(1)} %get-tuple-element.192, f32[2,3,64,512]{2,1,3,0:T(4,128)} %get-tuple-element.219, s32[]{:T(128)} %get-tuple-element.209, f32[64,512]{0,1:T(8,128)S(1)} %get-tuple-element.193), kind=kOutput, calls=%fused_computation.7.clone.1 | convolution fusion | flops 43089920 | bytes 1638912 | tf_op jit(solution)/shard_map/while/body/eval_jaxpr/ceb,enb->bcn/dot_general | solution.py:73
  94.8 14.0 %fusion.67 = f32[512,1,32]{2,1,0:T(1,128)S(1)} fusion(f32[64,512,1]{0,2,1:T(1,128)S(1)} %bitcast.118, s32[64,512]{0,1:T(8,128)S(1)} %get-tuple-element.191, s32[64,512]{0,1:T(8,128)S(1)} %get-tuple-element.192), kind=kOutput, calls=%fused_computation.8.clone.1 | convolution fusion | flops 17825792 | bytes 458752 | tf_op jit(solution)/shard_map/while/body/eval_jaxpr/eb,enb->bn/dot_general | solution.py:74
  110.3 4.5 %scatter_custom_fusion.1 = f32[2048,128]{1,0:T(8,128)} fusion(s32[1024]{0:T(1024)S(1)} %bitcast.132, f32[1024,128]{1,0:T(8,128)} %bitcast.136, f32[]{:T(128)} %constant.34.clone.1), kind=kCustom, calls=%fused_computation.90 | custom fusion | bytes 1049088 | tf_op jit(solution)/shard_map/scatter | solution.py:129
  114.8 5.8 %all-to-all-start.1 = ((f32[32,64,128]{2,1,0:T(8,128)}), f32[32,64,128]{2,1,0:T(8,128)S(1)}, u32[]{:S(2)}, u32[]{:S(2)}) async-start(f32[32,64,128]{2,1,0:T(8,128)} %bitcast.34), calls=%async_computation.1 | async-start | bytes 2097152 | tf_op jit(solution)/shard_map/all_to_all | solution.py:131
  122.0 24.9 %all-to-all-done.1 = f32[32,64,128]{2,1,0:T(8,128)S(1)} async-done(((f32[32,64,128]{2,1,0:T(8,128)}), f32[32,64,128]{2,1,0:T(8,128)S(1)}, u32[]{:S(2)}, u32[]{:S(2)}) %all-to-all-start.1) | async-done | bytes 1048608 | tf_op jit(solution)/shard_map/all_to_all | solution.py:131
  146.9 11.6 %scatter_custom_fusion.2 = f32[1025,128]{1,0:T(8,128)S(1)} fusion(s32[2048]{0:T(1024)S(1)} %bitcast.135, f32[2048,128]{1,0:T(8,128)S(1)} %bitcast.125, f32[]{:T(128)} %constant.34.clone.1), kind=kCustom, calls=%fused_computation.92 | custom fusion | flops 262144 | bytes 524804 | tf_op jit(solution)/shard_map/scatter-add | solution.py:149
  164.8 4.7 %collective-permute-start.1 = (f32[4,1,32,256]{3,2,1,0:T(8,128)S(1)}, f32[4,1,32,256]{3,2,1,0:T(8,128)S(1)}, u32[]{:S(2)}, u32[]{:S(2)}) collective-permute-start(f32[4,1,32,256]{3,2,1,0:T(8,128)S(1)} %get-tuple-element.124), channel_id=1, source_target_pairs={{1,0},{2,1},{3,2},{4,3},{5,4},{6,5},{7,6},{8,7},{9,8},{10,9},{11,1... | collective-permute-start | bytes 393224 | tf_op jit(solution)/shard_map/ppermute | solution.py:24
  173.9 5.3 %collective-permute-start.3 = (f32[4,1,32,256]{3,2,1,0:T(8,128)S(1)}, f32[4,1,32,256]{3,2,1,0:T(8,128)S(1)}, u32[]{:S(2)}, u32[]{:S(2)}) collective-permute-start(f32[4,1,32,256]{3,2,1,0:T(8,128)S(1)} %get-tuple-element.122), channel_id=1, source_target_pairs={{1,0},{2,1},{3,2},{4,3},{5,4},{6,5},{7,6},{8,7},{9,8},{10,9},{11,1... | collective-permute-start | bytes 393224 | tf_op jit(solution)/shard_map/ppermute | solution.py:24
  182.4 5.4 %collective-permute-start.5 = (f32[4,1,32,256]{3,2,1,0:T(8,128)S(1)}, f32[4,1,32,256]{3,2,1,0:T(8,128)S(1)}, u32[]{:S(2)}, u32[]{:S(2)}) collective-permute-start(f32[4,1,32,256]{3,2,1,0:T(8,128)S(1)} %get-tuple-element.120), channel_id=1, source_target_pairs={{1,0},{2,1},{3,2},{4,3},{5,4},{6,5},{7,6},{8,7},{9,8},{10,9},{11,1... | collective-permute-start | bytes 393224 | tf_op jit(solution)/shard_map/ppermute | solution.py:24
  196.0 7.6 %gather_fusion = f32[2048,128]{1,0:T(8,128)} fusion(f32[1024,128]{1,0:T(8,128)S(1)} %copy.50, s32[2048]{0:T(1024)S(1)} %broadcast_clamp_fusion), kind=kCustom, calls=%fused_computation | custom fusion | bytes 2105344 | tf_op jit(solution)/shard_map/gather | solution.py:172
  203.6 5.8 %all-to-all-start.2 = ((f32[32,64,128]{2,1,0:T(8,128)}), f32[32,64,128]{2,1,0:T(8,128)S(1)}, u32[]{:S(2)}, u32[]{:S(2)}) async-start(f32[32,64,128]{2,1,0:T(8,128)} %bitcast.39), calls=%async_computation.2 | async-start | bytes 2097152 | tf_op jit(solution)/shard_map/all_to_all | solution.py:173
  209.4 26.2 %all-to-all-done.2 = f32[32,64,128]{2,1,0:T(8,128)S(1)} async-done(((f32[32,64,128]{2,1,0:T(8,128)}), f32[32,64,128]{2,1,0:T(8,128)S(1)}, u32[]{:S(2)}, u32[]{:S(2)}) %all-to-all-start.2) | async-done | bytes 1048608 | tf_op jit(solution)/shard_map/all_to_all | solution.py:173
  235.6 4.0 %gather_fusion.1 = f32[1024,128]{1,0:T(8,128)} fusion(f32[2048,128]{1,0:T(8,128)S(1)} %bitcast.115, s32[1024]{0:T(1024)S(1)} %broadcast_clamp_fusion.1), kind=kCustom, calls=%fused_computation.1 | custom fusion | bytes 1052672 | tf_op jit(solution)/shard_map/gather | solution.py:180
  241.7 41.4 %while.21 = (s32[]{:T(128)}, f32[2,64,512]{1,2,0:T(8,128)}, f32[2,3,64,512]{2,1,3,0:T(4,128)}, s32[2,2,64,512]{2,3,1,0:T(8,128)S(1)}, f32[2,512,4,32]{3,2,1,0:T(4,128)S(1)}, /*index=5*/s32[]{:T(128)}, s32[]{:T(128)}, s32[]{}) while((s32[]{:T(128)}, f32[2,64,512]{1,2,0:T(8,128)}, f32[2,3,64,512]{2,1,3,0:T(4,128)}, ...), condition=%wide.region_10.11_spmd, body=%wide.region_8.10_spmd.sunk | while | flops 61046784 | bytes 6685325 | solution.py:104
  243.5 9.2 %fusion.71 = f32[64,512]{0,1:T(8,128)S(1)} fusion(s32[64,512]{0,1:T(8,128)S(1)} %get-tuple-element.199, s32[64,512]{0,1:T(8,128)S(1)} %get-tuple-element.200, f32[512,4,32]{2,1,0:T(4,128)S(1)} %dynamic-slice_bitcast_fusion.10, f32[2,3,64,512]{2,1,3,0:T(4,128)S(1)} %copy-done.1, s32[]{:T(128)} %get-tuple-element.233), kind=kOutput, calls=%fused_computation.37.clone.1 | convolution fusion | flops 43155456 | bytes 1048580 | tf_op jit(solution)/shard_map/while/body/eval_jaxpr/bcn,enb->ceb/dot_general | solution.py:96
  252.7 9.1 %fusion.70 = f32[512,1,64]{2,1,0:T(1,128)S(1)} fusion(s32[64,512]{0,1:T(8,128)S(1)} %get-tuple-element.199, s32[64,512]{0,1:T(8,128)S(1)} %get-tuple-element.200, f32[512,4,32]{2,1,0:T(4,128)S(1)} %dynamic-slice_bitcast_fusion.10), kind=kOutput, calls=%fused_computation.28.clone.1 | convolution fusion | flops 17825792 | bytes 917504 | tf_op jit(solution)/shard_map/while/body/eval_jaxpr/bn,enb->eb/dot_general | solution.py:99
  264.1 9.2 %fusion.71 = f32[64,512]{0,1:T(8,128)S(1)} fusion(s32[64,512]{0,1:T(8,128)S(1)} %get-tuple-element.199, s32[64,512]{0,1:T(8,128)S(1)} %get-tuple-element.200, f32[512,4,32]{2,1,0:T(4,128)S(1)} %dynamic-slice_bitcast_fusion.10, f32[2,3,64,512]{2,1,3,0:T(4,128)S(1)} %copy-done.1, s32[]{:T(128)} %get-tuple-element.233), kind=kOutput, calls=%fused_computation.37.clone.1 | convolution fusion | flops 43155456 | bytes 1048580 | tf_op jit(solution)/shard_map/while/body/eval_jaxpr/bcn,enb->ceb/dot_general | solution.py:96
  273.3 9.1 %fusion.70 = f32[512,1,64]{2,1,0:T(1,128)S(1)} fusion(s32[64,512]{0,1:T(8,128)S(1)} %get-tuple-element.199, s32[64,512]{0,1:T(8,128)S(1)} %get-tuple-element.200, f32[512,4,32]{2,1,0:T(4,128)S(1)} %dynamic-slice_bitcast_fusion.10), kind=kOutput, calls=%fused_computation.28.clone.1 | convolution fusion | flops 17825792 | bytes 917504 | tf_op jit(solution)/shard_map/while/body/eval_jaxpr/bn,enb->eb/dot_general | solution.py:99
  (106 shorter events, 45.5 us)
Async XLA Ops:
  0.0 26.9 %copy-start.4 = (s32[2,64,1024]{2,1,0:T(8,128)S(1)}, s32[2,64,1024]{2,1,0:T(8,128)}, u32[]{:S(2)}) copy-start(s32[2,64,1024]{2,1,0:T(8,128)} %param.15) | copy-start | bytes 1572868
  11.7 98.7 %copy-start.5 = (s32[1024,1]{0,1:T(1,128)}, s32[1024,1]{0,1:T(1,128)S(1)}, u32[]{:S(2)}) copy-start(s32[1024,1]{0,1:T(1,128)S(1)} %compare_select_fusion.2) | copy-start | bytes 12292
  16.9 98.0 %all-to-all-start = ((s32[32,1,64]{2,1,0:T(1,128)}), s32[32,1,64]{2,1,0:T(1,128)S(1)}, u32[]{:S(2)}, u32[]{:S(2)}) async-start(s32[32,1,64]{2,1,0:T(1,128)} %all_to_all.12), calls=%async_computation | async-start | bytes 32768 | tf_op jit(solution)/shard_map/all_to_all | solution.py:138
  24.2 3.5 %copy-start.3 = (f32[64,1024]{1,0:T(8,128)S(1)}, f32[64,1024]{1,0:T(8,128)}, u32[]{:S(2)}) copy-start(f32[64,1024]{1,0:T(8,128)} %param.12) | copy-start | bytes 786436
  62.8 14.3 %copy-start.12 = (f32[2,512,128]{2,1,0:T(8,128)S(1)}, f32[2,512,128]{2,1,0:T(8,128)}, u32[]{:S(2)}) copy-start(f32[2,512,128]{2,1,0:T(8,128)} %get-tuple-element.210) | copy-start | bytes 1572868 | tf_op jit(solution)/shard_map/while
  94.8 14.3 %copy-start.12 = (f32[2,512,128]{2,1,0:T(8,128)S(1)}, f32[2,512,128]{2,1,0:T(8,128)}, u32[]{:S(2)}) copy-start(f32[2,512,128]{2,1,0:T(8,128)} %get-tuple-element.210) | copy-start | bytes 1572868 | tf_op jit(solution)/shard_map/while
  114.8 32.1 %all-to-all-start.1 = ((f32[32,64,128]{2,1,0:T(8,128)}), f32[32,64,128]{2,1,0:T(8,128)S(1)}, u32[]{:S(2)}, u32[]{:S(2)}) async-start(f32[32,64,128]{2,1,0:T(8,128)} %bitcast.34), calls=%async_computation.1 | async-start | bytes 2097152 | tf_op jit(solution)/shard_map/all_to_all | solution.py:131
  161.4 10.8 %copy-start.2 = (f32[4,32,256]{2,1,0:T(8,128)S(1)}, f32[4,32,256]{2,1,0:T(8,128)}, u32[]{:S(2)}) copy-start(f32[4,32,256]{2,1,0:T(8,128)} %param.18) | copy-start | bytes 393220
  161.4 10.8 %copy-start.7 = (f32[4]{0:T(128)S(1)}, f32[4]{0:T(128)}, u32[]{:S(2)}) copy-start(f32[4]{0:T(128)} %constant.74.clone) | copy-start | bytes 52
  161.4 10.8 %copy-start.9 = (f32[4]{0:T(128)S(1)}, f32[4]{0:T(128)}, u32[]{:S(2)}) copy-start(f32[4]{0:T(128)} %constant.96) | copy-start | bytes 52
  162.8 19.0 %copy-start = (f32[4,4,32,256]{3,2,1,0:T(8,128)S(1)}, f32[4,4,32,256]{3,2,1,0:T(8,128)}, u32[]{:S(2)}) copy-start(f32[4,4,32,256]{3,2,1,0:T(8,128)} %reshape.161) | copy-start | bytes 1572868
  162.8 19.0 %copy-start.11 = (f32[4]{0:T(128)S(1)}, f32[4]{0:T(128)}, u32[]{:S(2)}) copy-start(f32[4]{0:T(128)} %constant.97) | copy-start | bytes 52
  164.1 8.1 %collective-permute-start = (f32[4,1,32,256]{3,2,1,0:T(8,128)S(1)}, f32[4,1,32,256]{3,2,1,0:T(8,128)S(1)}, u32[]{:S(2)}, u32[]{:S(2)}) collective-permute-start(f32[4,1,32,256]{3,2,1,0:T(8,128)S(1)} %get-tuple-element.123), channel_id=1, source_target_pairs={{0,1},{1,2},{2,3},{3,4},{4,5},{5,6},{6,7},{7,8},{8,9},{9,10},{10,1... | collective-permute-start | bytes 393224 | tf_op jit(solution)/shard_map/ppermute | solution.py:22
  164.8 7.4 %collective-permute-start.1 = (f32[4,1,32,256]{3,2,1,0:T(8,128)S(1)}, f32[4,1,32,256]{3,2,1,0:T(8,128)S(1)}, u32[]{:S(2)}, u32[]{:S(2)}) collective-permute-start(f32[4,1,32,256]{3,2,1,0:T(8,128)S(1)} %get-tuple-element.124), channel_id=1, source_target_pairs={{1,0},{2,1},{3,2},{4,3},{5,4},{6,5},{7,6},{8,7},{9,8},{10,9},{11,1... | collective-permute-start | bytes 393224 | tf_op jit(solution)/shard_map/ppermute | solution.py:24
  173.8 16.6 %copy-start.8 = (f32[4]{0:T(128)S(1)}, f32[4]{0:T(128)}, u32[]{:S(2)}) copy-start(f32[4]{0:T(128)} %constant.74.clone) | copy-start | bytes 52
  173.8 16.6 %copy-start.10 = (f32[4]{0:T(128)S(1)}, f32[4]{0:T(128)}, u32[]{:S(2)}) copy-start(f32[4]{0:T(128)} %constant.96) | copy-start | bytes 52
  173.8 8.0 %collective-permute-start.2 = (f32[4,1,32,256]{3,2,1,0:T(8,128)S(1)}, f32[4,1,32,256]{3,2,1,0:T(8,128)S(1)}, u32[]{:S(2)}, u32[]{:S(2)}) collective-permute-start(f32[4,1,32,256]{3,2,1,0:T(8,128)S(1)} %get-tuple-element.121), channel_id=1, source_target_pairs={{0,1},{1,2},{2,3},{3,4},{4,5},{5,6},{6,7},{7,8},{8,9},{9,10},{10,1... | collective-permute-start | bytes 393224 | tf_op jit(solution)/shard_map/ppermute | solution.py:22
  173.9 8.0 %collective-permute-start.3 = (f32[4,1,32,256]{3,2,1,0:T(8,128)S(1)}, f32[4,1,32,256]{3,2,1,0:T(8,128)S(1)}, u32[]{:S(2)}, u32[]{:S(2)}) collective-permute-start(f32[4,1,32,256]{3,2,1,0:T(8,128)S(1)} %get-tuple-element.122), channel_id=1, source_target_pairs={{1,0},{2,1},{3,2},{4,3},{5,4},{6,5},{7,6},{8,7},{9,8},{10,9},{11,1... | collective-permute-start | bytes 393224 | tf_op jit(solution)/shard_map/ppermute | solution.py:24
  182.4 8.0 %collective-permute-start.4 = (f32[4,1,32,256]{3,2,1,0:T(8,128)S(1)}, f32[4,1,32,256]{3,2,1,0:T(8,128)S(1)}, u32[]{:S(2)}, u32[]{:S(2)}) collective-permute-start(f32[4,1,32,256]{3,2,1,0:T(8,128)S(1)} %get-tuple-element.119), channel_id=1, source_target_pairs={{0,1},{1,2},{2,3},{3,4},{4,5},{5,6},{6,7},{7,8},{8,9},{9,10},{10,1... | collective-permute-start | bytes 393224 | tf_op jit(solution)/shard_map/ppermute | solution.py:22
  182.4 8.0 %collective-permute-start.5 = (f32[4,1,32,256]{3,2,1,0:T(8,128)S(1)}, f32[4,1,32,256]{3,2,1,0:T(8,128)S(1)}, u32[]{:S(2)}, u32[]{:S(2)}) collective-permute-start(f32[4,1,32,256]{3,2,1,0:T(8,128)S(1)} %get-tuple-element.120), channel_id=1, source_target_pairs={{1,0},{2,1},{3,2},{4,3},{5,4},{6,5},{7,6},{8,7},{9,8},{10,9},{11,1... | collective-permute-start | bytes 393224 | tf_op jit(solution)/shard_map/ppermute | solution.py:24
  203.6 5.8 %copy-start.6 = (s32[1024,1]{0,1:T(1,128)S(1)}, s32[1024,1]{0,1:T(1,128)}, u32[]{:S(2)}) copy-start(s32[1024,1]{0,1:T(1,128)} %copy-done.5) | copy-start | bytes 12292
  203.6 32.0 %all-to-all-start.2 = ((f32[32,64,128]{2,1,0:T(8,128)}), f32[32,64,128]{2,1,0:T(8,128)S(1)}, u32[]{:S(2)}, u32[]{:S(2)}) async-start(f32[32,64,128]{2,1,0:T(8,128)} %bitcast.39), calls=%async_computation.2 | async-start | bytes 2097152 | tf_op jit(solution)/shard_map/all_to_all | solution.py:173
  241.9 1.6 copy-start.1
  262.5 1.6 copy-start.1
  (2 other events, 1.6 us)
where the time goes:
time: 281 us; the launch traced here: 286 us
  matrix products  95.5 us (34%)
  waiting for transfers between devices  59.1 us (21%)
  local copies, waits for them, and re-layouts  44.6 us (16%)
  starting transfers between devices  35.1 us (12%)
  other arithmetic  33.3 us (12%)
  loops' own time  18.1 us (6%)
    dot_general x2, matrix products, block_one_group(): jnp.einsum('ceb,enb->bcn', vector_part, head_hot + tail_hot, precision=hi...  30.9 us
    dot_general x2, matrix products, block_one_group(): jnp.einsum('eb,enb->bn', resid_part, head_hot - tail_hot, precision=highest)  28.1 us
    all_to_all x1, waiting for transfers between devices, per_device(): lax.all_to_all(outgoing.reshape(devices, capacity, width), ('edge', 'node...  26.2 us
    all_to_all x1, waiting for transfers between devices, per_device(): lax.all_to_all(partials.reshape(devices, capacity, width), ('edge', 'node...  24.9 us
    dot_general x2, matrix products, lift_one_group(): jnp.einsum('bcn,enb->ceb', value_part[:, :3], head_hot + tail_hot, precis...  18.3 us
    dot_general x2, matrix products, lift_one_group(): jnp.einsum('bn,enb->eb', value_part[:, 3], head_hot - tail_hot, precision...  18.2 us
    another operation x1, loops' own time, block_terms(): lax.map(block_one_group, (group_last(residual, group_size), group_last(ta...  17.8 us
    ppermute x3, starting transfers between devices, with_halo(): lax.ppermute(head, axis, [((i + 1) % count, i) for i in range(count)])  15.4 us
  transfers between devices with their start and end apart: 9, of which 5 were waited for; matrix products, arithmetic and copies ran while one was open for 25% of the time, Pallas kernels for 0%

commit v1 on v0

v1 whole, which is shorter than its diff:
```python
import functools

import jax
import jax.numpy as jnp
from jax import lax
from jax.experimental import pallas as pl
from jax.experimental.pallas import tpu as pltpu
from jax.sharding import PartitionSpec as P

BLOCK_EDGES = 64
NODE_BLOCK = 32
LANES = 128
GROUP = 256

F32 = jnp.float32
BF16 = jnp.bfloat16
MESH = pl.DeviceIdType.MESH


def halves(values):
    high = values.astype(BF16)
    low = (values - high.astype(F32)).astype(BF16)
    return high, low


def hot(mask):
    return jnp.where(mask, 1.0, 0.0).astype(BF16)


def dot(a, b):
    return jnp.dot(a, b, preferred_element_type=F32)


def folded(product):
    return product[:, :LANES] + product[:, LANES:]


def order_of(groups):
    return [(groups // 2 + 3 * k) % groups for k in range(groups)]


def kernel(
    n,
    n_node,
    slices,
    rows_radial,
    resid_ref,
    tangent_ref,
    jacobi_ref,
    ends_ref,
    target_ref,
    label_ref,
    diag_ref,
    out_ref,
    pos_ref,
    posb_ref,
    lab_out,
    lab_in,
    labb_ref,
    rows_ref,
    send_ref,
    got_ref,
    acc_ref,
    rest_ref,
    field_ref,
    sol_ref,
    back_ref,
    ret_ref,
    lab_send,
    lab_recv,
    go_send,
    go_recv,
    back_send,
    back_recv,
    halo_send,
    halo_recv,
):
    me = lax.axis_index("edge") * n_node + lax.axis_index("node")
    blocks = resid_ref.shape[1]
    lane_groups = blocks // LANES
    cap = 2 * blocks // n
    peers = GROUP // cap
    per_row = LANES // cap
    groups = n // peers
    my_group = me // peers
    my_place = lax.rem(me, peers)
    slab = rows_radial * 8
    nodal = slices * slab
    order = order_of(groups)

    def device(t):
        return (t // n_node, lax.rem(t, n_node))

    def to_group(step):
        return lax.rem(my_group + step, groups)

    def from_group(step):
        return lax.rem(my_group + groups - step, groups)

    def partner(group, turn):
        return group * peers + lax.rem(my_place + turn, peers)

    barrier = pltpu.get_barrier_semaphore()
    for step in range(1, n):
        pl.semaphore_signal(
            barrier, inc=1, device_id=device(lax.rem(me + step, n)), device_id_type=MESH
        )

    upper = hot(
        lax.broadcasted_iota(jnp.int32, (LANES, LANES), 0)
        <= lax.broadcasted_iota(jnp.int32, (LANES, LANES), 1)
    )
    device_ids = lax.broadcasted_iota(jnp.int32, (n, LANES), 0)
    slot_ids = lax.broadcasted_iota(jnp.int32, (LANES, LANES), 0)
    carry = jnp.zeros((n, 1), F32)
    label_sum = jnp.zeros((2 * n, LANES), F32)
    offset = lax.rem(me, per_row) * cap
    for g in range(lane_groups):
        cols = slice(g * LANES, (g + 1) * LANES)
        named = target_ref[:, cols]
        match = jnp.where(device_ids == named, 1.0, 0.0)
        local = dot(match.astype(BF16), upper)
        rank = jnp.sum(match * (local + carry), axis=0, keepdims=True) - 1.0
        carry = carry + local[:, LANES - 1 :]
        place = named * cap + rank.astype(jnp.int32)
        pos_ref[:, cols] = place
        posb_ref[cols, :] = jnp.broadcast_to(place.astype(F32), (LANES, LANES)).T
        mark = label_ref[:, cols] + 1
        high = match * (mark >> 5).astype(F32)
        low = match * (mark & 31).astype(F32)
        slots = hot(slot_ids == rank.astype(jnp.int32) + offset)
        label_sum = label_sum + lax.dot_general(
            jnp.concatenate([high, low], axis=0).astype(BF16),
            slots,
            (((1,), (1,)), ((), ())),
            preferred_element_type=F32,
        )
    labels = 32.0 * label_sum[:n] + label_sum[n:]
    for t in range(n):
        lab_out[t] = labels[t : t + 1]

    pl.semaphore_wait(barrier, n - 1)

    lab_in[me] = lab_out[me]
    for step in range(1, n):
        t = lax.rem(me + step, n)
        pltpu.make_async_remote_copy(
            src_ref=lab_out.at[t],
            dst_ref=lab_in.at[me],
            send_sem=lab_send,
            recv_sem=lab_recv,
            device_id=device(t),
            device_id_type=MESH,
        ).start()

    node_ids = lax.broadcasted_iota(jnp.int32, (NODE_BLOCK, LANES), 0)

    def terms_of(g, _):
        cols = pl.ds(pl.multiple_of(g * LANES, LANES), LANES)

        def chunk(k, sums):
            rows = pl.ds(pl.multiple_of(k * 8, 8), 8)
            residual = resid_ref[rows, cols]
            halved = 0.5 * residual
            vectors = [tangent_ref[c, rows, cols] * halved for c in range(3)]
            tails = ends_ref[0, rows, cols]
            heads = ends_ref[1, rows, cols]
            sums = list(sums)
            for e in range(8):
                at_tail = node_ids == tails[e : e + 1]
                at_head = node_ids == heads[e : e + 1]
                either = at_tail | at_head
                for c in range(3):
                    sums[c] = sums[c] + jnp.where(either, vectors[c][e : e + 1], 0.0)
                value = residual[e : e + 1]
                sums[3] = sums[3] + jnp.where(at_head, value, jnp.where(at_tail, -value, 0.0))
            return tuple(sums)

        zero = jnp.zeros((NODE_BLOCK, LANES), F32)
        sums = lax.fori_loop(0, BLOCK_EDGES // 8, chunk, (zero,) * 4)
        high, low = halves(jnp.concatenate(sums, axis=0).T)
        rows_ref[cols, :LANES] = high
        rows_ref[cols, LANES:] = low
        return 0

    lax.fori_loop(0, lane_groups, terms_of, 0)

    def rows_copy(src, dst, sends, recvs, step, turn):
        t = partner(to_group(step), turn)
        return pltpu.make_async_remote_copy(
            src_ref=src.at[pl.ds(pl.multiple_of(t * cap, cap), cap)],
            dst_ref=dst.at[pl.ds(pl.multiple_of(me * cap, cap), cap)],
            send_sem=sends.at[step],
            recv_sem=recvs.at[step],
            device_id=device(t),
            device_id_type=MESH,
        )

    def group_copy(src, dst, sends, recvs, step):
        size = GROUP if step else GROUP - cap
        return pltpu.make_async_remote_copy(
            src_ref=src.at[pl.ds(0, size)],
            dst_ref=dst.at[pl.ds(0, size)],
            send_sem=sends.at[step],
            recv_sem=recvs.at[step],
            device_id=device(me),
            device_id_type=MESH,
        )

    def send_group(src, dst, sends, recvs, step):
        for turn in range(peers):
            if step == 0 and turn == 0:
                mine = pl.ds(pl.multiple_of(me * cap, cap), cap)
                dst[mine, :] = src[mine, :]
            else:
                rows_copy(src, dst, sends, recvs, step, turn).start()

    for step in order:
        base = pl.multiple_of(to_group(step) * GROUP, GROUP)
        ids = lax.broadcasted_iota(jnp.int32, (GROUP, blocks), 0) + base
        send_ref[pl.ds(base, GROUP), :] = folded(dot(hot(pos_ref[...] == ids), rows_ref[...]))
        send_group(send_ref, got_ref, go_send, go_recv, step)

    pltpu.make_async_remote_copy(
        src_ref=lab_out.at[pl.ds(0, n - 1)],
        dst_ref=lab_in.at[pl.ds(0, n - 1)],
        send_sem=lab_send,
        recv_sem=lab_recv,
        device_id=device(me),
        device_id_type=MESH,
    ).wait()

    def label_row(first):
        total = lab_in[first]
        for k in range(1, per_row):
            total = total + lab_in[first + k]
        return total

    for k in range(2 * groups):
        row = label_row(k * per_row)
        labb_ref[k * LANES : (k + 1) * LANES, :] = jnp.broadcast_to(row, (LANES, LANES)).T

    block_ids = (lax.broadcasted_iota(jnp.int32, (nodal, LANES), 0) + 1).astype(F32)
    for k, step in enumerate(order):
        group_copy(send_ref, got_ref, go_send, go_recv, step).wait_recv()
        source = from_group(step)
        chosen = jnp.concatenate(
            [
                hot(block_ids == label_row(source * peers)),
                hot(block_ids == label_row(source * peers + per_row)),
            ],
            axis=1,
        )
        base = pl.multiple_of(source * GROUP, GROUP)
        high, low = halves(got_ref[pl.ds(base, GROUP), :])
        part = folded(dot(chosen, jnp.concatenate([high, low], axis=1)))
        acc_ref[...] = part if k == 0 else acc_ref[...] + part

    lane = lax.broadcasted_iota(jnp.int32, (1, LANES), 1)
    scale = jnp.where(lane < 3 * NODE_BLOCK, 1.0, 0.5).astype(F32)
    top = 12.0 + 8.0 * scale
    bottom = top / 8.0
    centre = (top + bottom) / 2.0
    radius = (top - bottom) / 2.0
    ratio = centre / radius
    first = 1.0 / ratio
    second = 1.0 / (2.0 * ratio - first)
    coef_one = second * first
    coef_two = 2.0 * second / radius
    inverse = 1.0 / centre

    inner = lax.broadcasted_iota(jnp.int32, (slab, LANES), 0) & 7
    node = lax.broadcasted_iota(jnp.int32, (slab, LANES), 1) & (NODE_BLOCK - 1)
    last_node = node == NODE_BLOCK - 1
    first_node = node == 0
    last_inner = inner == 7
    first_inner = inner == 0
    edge_zero = jnp.zeros((8, LANES), F32)
    left = lax.rem(me + n - 1, n)
    right = lax.rem(me + 1, n)

    def own(s):
        return slice(s * slab, (s + 1) * slab)

    def stored(s):
        return slice((s + 1) * slab, (s + 2) * slab)

    def halo(level, side):
        at = stored(0) if side == 0 else stored(slices - 1)
        to = stored(slices) if side == 0 else own(0)
        return pltpu.make_async_remote_copy(
            src_ref=field_ref.at[level, at],
            dst_ref=field_ref.at[level, to],
            send_sem=halo_send.at[level, side],
            recv_sem=halo_recv.at[level, side],
            device_id=device(left if side == 0 else right),
            device_id_type=MESH,
        )

    def applied(level, s):
        field = field_ref.at[level]
        here = field[stored(s)]
        beside = field[own(s)] + field[stored(s + 1)]
        beside = beside + jnp.concatenate([edge_zero, here[:-8]], axis=0)
        beside = beside + jnp.concatenate([here[8:], edge_zero], axis=0)
        after = pltpu.roll(pltpu.roll(here, slab - 1, 0), NODE_BLOCK - 1, 1)
        after = jnp.where(last_inner, 0.0, after)
        before = pltpu.roll(pltpu.roll(here, 1, 0), LANES - NODE_BLOCK + 1, 1)
        before = jnp.where(first_inner, 0.0, before)
        beside = beside + jnp.where(last_node, after, pltpu.roll(here, LANES - 1, 1))
        beside = beside + jnp.where(first_node, before, pltpu.roll(here, 1, 1))
        return diag_ref[own(s)] * here - beside

    outer = [0, slices - 1]
    middle = list(range(1, slices - 1))

    def stage(level, body):
        if level:
            for side in range(2):
                halo(level - 1, side).wait_recv()
        for s in outer:
            body(s)
        if level < 3:
            for side in range(2):
                halo(level, side).start()
        for s in middle:
            body(s)

    def begin(s):
        field_ref[0, stored(s)] = acc_ref[own(s)] * inverse

    def sweep(s):
        rest = acc_ref[own(s)] - applied(0, s)
        step = field_ref[0, stored(s)]
        field_ref[1, stored(s)] = step + (coef_one * step + coef_two * rest)

    def residue(s):
        rest = acc_ref[own(s)] - applied(1, s)
        rest_ref[own(s)] = rest
        field_ref[2, stored(s)] = rest * inverse

    def finish(s):
        step = field_ref[2, stored(s)]
        rest = rest_ref[own(s)] - applied(2, s)
        total = (field_ref[1, stored(s)] + step) + (coef_one * step + coef_two * rest)
        high, low = halves(total)
        sol_ref[own(s), :LANES] = high
        sol_ref[own(s), LANES:] = low

    for level, body in enumerate((begin, sweep, residue, finish)):
        stage(level, body)

    lane_ids = lax.broadcasted_iota(jnp.int32, (GROUP, LANES), 1).astype(F32)
    for step in order:
        base = pl.multiple_of(to_group(step) * GROUP, GROUP)
        marks = labb_ref[pl.ds(base, GROUP), :] - 1.0
        chosen = jnp.concatenate(
            [hot(marks == lane_ids + float(k * LANES)) for k in range(nodal // LANES)], axis=1
        )
        back_ref[pl.ds(base, GROUP), :] = folded(dot(chosen, sol_ref[...]))
        send_group(back_ref, ret_ref, back_send, back_recv, step)

    slot_lanes = lax.broadcasted_iota(jnp.int32, (blocks, LANES), 1)
    for k, step in enumerate(order):
        group_copy(back_ref, ret_ref, back_send, back_recv, step).wait_recv()
        base = pl.multiple_of(from_group(step) * GROUP, GROUP)
        places = posb_ref[...].astype(jnp.int32) - base
        chosen = jnp.concatenate(
            [hot(places == slot_lanes), hot(places == slot_lanes + LANES)], axis=1
        )
        high, low = halves(ret_ref[pl.ds(base, GROUP), :])
        part = folded(dot(chosen, jnp.concatenate([high, low], axis=1)))
        acc_ref[...] = part if k == 0 else acc_ref[...] + part

    def lift(g, _):
        cols = pl.ds(pl.multiple_of(g * LANES, LANES), LANES)
        values = acc_ref[cols, :].T

        for k in range(BLOCK_EDGES // 8):
            rows = slice(k * 8, k * 8 + 8)

            def taken(c, ids, part):
                found = None
                for piece in range(NODE_BLOCK // 8):
                    start = c * NODE_BLOCK + piece * 8
                    here = jnp.take_along_axis(
                        values[start : start + 8], ids, axis=0, mode="promise_in_bounds"
                    )
                    found = here if piece == 0 else jnp.where(part == piece, here, found)
                return found

            tails = ends_ref[0, rows, cols]
            heads = ends_ref[1, rows, cols]
            tail_at, tail_part = tails & 7, tails >> 3
            head_at, head_part = heads & 7, heads >> 3
            total = None
            for c in range(3):
                pair = taken(c, head_at, head_part) + taken(c, tail_at, tail_part)
                term = tangent_ref[c, rows, cols] * pair
                total = term if c == 0 else total + term
            drop = taken(3, head_at, head_part) - taken(3, tail_at, tail_part)
            out_ref[rows, cols] = (
                jacobi_ref[rows, cols] * resid_ref[rows, cols] + 0.5 * total + drop
            )
        return 0

    lax.fori_loop(0, lane_groups, lift, 0)

    for step in order:
        group_copy(send_ref, got_ref, go_send, go_recv, step).wait_send()
        group_copy(back_ref, ret_ref, back_send, back_recv, step).wait_send()
    for level in range(3):
        for side in range(2):
            halo(level, side).wait_send()


def per_device(n, n_node, residual, tangent, jacobi, ends, target, node_block, sigma):
    blocks = residual.shape[1]
    slices, rows_radial, rows_axial = sigma.shape
    nodal = slices * rows_radial * rows_axial // NODE_BLOCK
    slab = nodal // slices
    slots = 2 * blocks
    width = 4 * NODE_BLOCK
    cells = sigma.reshape(nodal, NODE_BLOCK)
    diag = 6.0 + jnp.concatenate([cells, cells, cells, 0.5 * cells], axis=1)
    groups = slots // GROUP
    vmem = pl.BlockSpec(memory_space=pltpu.VMEM)
    return pl.pallas_call(
        functools.partial(kernel, n, n_node, slices, rows_radial),
        out_shape=jax.ShapeDtypeStruct(residual.shape, F32),
        in_specs=[vmem] * 7,
        out_specs=vmem,
        scratch_shapes=[
            pltpu.VMEM((1, blocks), jnp.int32),
            pltpu.VMEM((blocks, LANES), F32),
            pltpu.VMEM((n, 1, LANES), F32),
            pltpu.VMEM((n, 1, LANES), F32),
            pltpu.VMEM((slots, LANES), F32),
            pltpu.VMEM((blocks, 2 * width), BF16),
            pltpu.VMEM((slots, width), F32),
            pltpu.VMEM((slots, width), F32),
            pltpu.VMEM((nodal, width), F32),
            pltpu.VMEM((nodal, width), F32),
            pltpu.VMEM((3, nodal + 2 * slab, width), F32),
            pltpu.VMEM((nodal, 2 * width), BF16),
            pltpu.VMEM((slots, width), F32),
            pltpu.VMEM((slots, width), F32),
            pltpu.SemaphoreType.DMA,
            pltpu.SemaphoreType.DMA,
            pltpu.SemaphoreType.DMA((groups,)),
            pltpu.SemaphoreType.DMA((groups,)),
            pltpu.SemaphoreType.DMA((groups,)),
            pltpu.SemaphoreType.DMA((groups,)),
            pltpu.SemaphoreType.DMA((3, 2)),
            pltpu.SemaphoreType.DMA((3, 2)),
        ],
        compiler_params=pltpu.CompilerParams(
            collective_id=0, has_side_effects=True, vmem_limit_bytes=48 * 1024 * 1024
        ),
    )(
        residual,
        tangent,
        jacobi,
        ends,
        target.reshape(1, blocks),
        node_block.reshape(1, blocks),
        diag,
    )


def solution(mesh):
    in_specs = (
        P(None, ("edge", "node")),
        P(None, None, ("edge", "node")),
        P(None, ("edge", "node")),
        P(None, None, ("edge", "node")),
        P(("edge", "node"), None),
        P(("edge", "node")),
        P(("edge", "node"), None, None),
    )
    out_specs = P(None, ("edge", "node"))
    n_node = mesh.shape["node"]
    n = mesh.shape["edge"] * n_node
    return jax.shard_map(
        functools.partial(per_device, n, n_node),
        mesh=mesh,
        in_specs=in_specs,
        out_specs=out_specs,
        check_vma=False,
    )
```

time: 281 us -> 81.1 us (0.29); the launches traced: 286 us -> 80.9 us
  matrix products: 95.5 us -> 0 us
  Pallas kernels: 0 us -> 77.7 us
  waiting for transfers between devices: 59.1 us -> 0 us
  local copies, waits for them, and re-layouts: 44.6 us -> 2.67 us
  starting transfers between devices: 35.1 us -> 0 us
  other arithmetic: 33.3 us -> 0.51 us
  loops' own time: 18.1 us -> 0 us
    dot_general x8 -> x0, matrix products: 95.5 us -> none  [the longest x2 30.9 us: block_one_group(): jnp.einsum('ceb,enb->bcn', vector_part, head_hot + tail_hot, precision=hi...]
    pallas_call x0 -> x1, Pallas kernels: none -> 77.7 us  [per_device(): pl.pallas_call(functools.partial(kernel, n, n_node, slices, rows_radial),...]
    all_to_all x3 -> x0, waiting for transfers between devices: 51.1 us -> none  [the longest x1 26.2 us: per_device(): lax.all_to_all(outgoing.reshape(devices, capacity, width), ('edge', 'node...]
    all_to_all x3 -> x0, starting transfers between devices: 18.9 us -> none  [the longest x1 7.3 us: per_device(): lax.all_to_all(labels.reshape(devices, capacity), ('edge', 'node'), split...]
    another operation x2 -> x0, loops' own time: 18.1 us -> none  [the longest x1 17.8 us: block_terms(): lax.map(block_one_group, (group_last(residual, group_size), group_last(ta...]
    ppermute x6 -> x0, starting transfers between devices: 16.2 us -> none  [the longest x3 15.4 us: with_halo(): lax.ppermute(head, axis, [((i + 1) % count, i) for i in range(count)])]
    gather x2 -> x0, local copies, waits for them, and re-layouts: 11.6 us -> none  [the longest x1 7.6 us: per_device(): outgoing = sol_blocks[jnp.clip(got_labels, 0, nodal_blocks - 1)]]
    scatter-add x1 -> x0, other arithmetic: 11.6 us -> none  [per_device(): jax.ops.segment_sum(got_terms, safe_labels, num_segments=nodal_blocks + 1)]
  transfers between devices with their start and end apart: 9 -> 0, of which waited for: 5 -> 0; matrix products, arithmetic and copies ran while one was open for 25% -> 0% of each run, Pallas kernels for 0% -> 0%
where the time goes in v1:
time: 81.1 us; the launch traced here: 80.9 us
  Pallas kernels  77.7 us (96%)
  local copies, waits for them, and re-layouts  2.67 us (3%)
    pallas_call x1, Pallas kernels, per_device(): pl.pallas_call(functools.partial(kernel, n, n_node, slices, rows_radial),...  77.7 us

profile of v1, /device:TPU:0, one launch (start us, length us, event | category | flops | bytes accessed | tf_op | source)
XLA Modules:
  0.0 80.9 jit_solution(10059438616550631277)
XLA Ops:
  0.0 1.1 %reshape.11 = f32[1024,32]{1,0:T(8,128)S(1)} reshape(f32[4,32,256]{2,1,0:T(8,128)} %param.13) | data formatting | bytes 262144 | tf_op jit(solution)/shard_map/reshape | solution.py:424
  1.1 0.0 copy-start.3
  1.1 0.0 copy-start.4
  1.1 0.0 copy-start.5
  1.2 0.0 copy-start
  1.2 0.0 copy-start.1
  1.2 0.0 copy-start.2
  1.2 0.5 maximum_add_fusion.diag_ref
  1.7 0.4 copy-done.3
  2.0 0.0 copy-done.4
  2.0 0.0 copy-done.5
  2.0 0.3 copy-done
  2.3 0.1 copy-done.1
  2.5 0.1 copy-done.2
  2.5 77.7 %shard_map.73 = f32[64,1024]{1,0:T(8,128)S(1)} custom-call(f32[64,1024]{1,0:T(8,128)S(1)} %copy-done.2, f32[3,64,1024]{2,1,0:T(8,128)S(1)} %copy-done, f32[64,1024]{1,0:T(8,128)S(1)} %copy-done.3, s32[2,64,1024]{2,1,0:T(8,128)S(1)} %copy-done.1, s32[1,1024]{1,0:T(1,128)S(1)} %bitcast.2, s32[1,1024]{1,0:T(1,128)S(1)} %bitcast.3, ...), custom_call_target="tpu_custom_call" | custom-call | tf_op jit(solution)/shard_map/pallas_call | solution.py:428
  80.2 0.7 copy.9
  (1 shorter events, 0.0 us)
Async XLA Ops:
  1.1 1.0 %copy-start.3 = (f32[64,1024]{1,0:T(8,128)S(1)}, f32[64,1024]{1,0:T(8,128)}, u32[]{:S(2)}) copy-start(f32[64,1024]{1,0:T(8,128)} %jacobi_ref.1) | copy-start | bytes 786436
  1.1 0.9 %copy-start.4 = (s32[1024,1]{0,1:T(1,128)S(1)}, s32[1024,1]{0,1:T(1,128)}, u32[]{:S(2)}) copy-start(s32[1024,1]{0,1:T(1,128)} %param.11) | copy-start | bytes 12292
  1.1 0.9 %copy-start.5 = (s32[1024]{0:T(1024)S(1)}, s32[1024]{0:T(1024)}, u32[]{:S(2)}) copy-start(s32[1024]{0:T(1024)} %param.12) | copy-start | bytes 12292
  1.2 1.2 %copy-start = (f32[3,64,1024]{2,1,0:T(8,128)S(1)}, f32[3,64,1024]{2,1,0:T(8,128)}, u32[]{:S(2)}) copy-start(f32[3,64,1024]{2,1,0:T(8,128)} %tangent_ref.1) | copy-start | bytes 2359300
  1.2 1.3 %copy-start.1 = (s32[2,64,1024]{2,1,0:T(8,128)S(1)}, s32[2,64,1024]{2,1,0:T(8,128)}, u32[]{:S(2)}) copy-start(s32[2,64,1024]{2,1,0:T(8,128)} %ends_ref.1) | copy-start | bytes 1572868
  1.2 1.4 %copy-start.2 = (f32[64,1024]{1,0:T(8,128)S(1)}, f32[64,1024]{1,0:T(8,128)}, u32[]{:S(2)}) copy-start(f32[64,1024]{1,0:T(8,128)} %resid_ref.1) | copy-start | bytes 786436

commit v2 on v1

v2 whole, which is shorter than its diff:
```python
import functools

import jax
import jax.numpy as jnp
from jax import lax
from jax.experimental import pallas as pl
from jax.experimental.pallas import tpu as pltpu
from jax.sharding import PartitionSpec as P

BLOCK_EDGES = 64
NODE_BLOCK = 32
LANES = 128
GROUP = 256

F32 = jnp.float32
BF16 = jnp.bfloat16
MESH = pl.DeviceIdType.MESH


def halves(values):
    high = values.astype(BF16)
    low = (values - high.astype(F32)).astype(BF16)
    return high, low


def hot(mask):
    return jnp.where(mask, 1.0, 0.0).astype(BF16)


def dot(a, b):
    return jnp.dot(a, b, preferred_element_type=F32)


def folded(product):
    return product[:, :LANES] + product[:, LANES:]


def order_of(groups):
    return [(groups // 2 + 3 * k) % groups for k in range(groups)]


def kernel(
    n,
    n_node,
    slices,
    resid_ref,
    tangent_ref,
    jacobi_ref,
    ends_ref,
    target_ref,
    label_ref,
    diag_ref,
    out_ref,
    pos_ref,
    posb_ref,
    lab_out,
    lab_in,
    labb_ref,
    rows_ref,
    send_ref,
    got_ref,
    acc_ref,
    rest_ref,
    field_ref,
    sol_ref,
    back_ref,
    ret_ref,
    mine_ref,
    lab_send,
    lab_recv,
    go_send,
    go_recv,
    back_send,
    back_recv,
    halo_send,
    halo_recv,
):
    me = lax.axis_index("edge") * n_node + lax.axis_index("node")
    blocks = resid_ref.shape[1]
    lane_groups = blocks // LANES
    cap = 2 * blocks // n
    deep = cap // 2
    peers = GROUP // cap
    groups = n // peers
    my_group = me // peers
    my_place = lax.rem(me, peers)
    slab = LANES
    nodal = slices * slab
    order = order_of(groups)

    def device(t):
        return (t // n_node, lax.rem(t, n_node))

    def to_group(step):
        return lax.rem(my_group + step, groups)

    def from_group(step):
        return lax.rem(my_group + groups - step, groups)

    def partner(group, turn):
        return group * peers + lax.rem(my_place + turn, peers)

    barrier = pltpu.get_barrier_semaphore()
    for step in range(1, n):
        pl.semaphore_signal(
            barrier, inc=1, device_id=device(lax.rem(me + step, n)), device_id_type=MESH
        )

    upper = hot(
        lax.broadcasted_iota(jnp.int32, (LANES, LANES), 0)
        <= lax.broadcasted_iota(jnp.int32, (LANES, LANES), 1)
    )
    device_ids = lax.broadcasted_iota(jnp.int32, (n, LANES), 0)
    slot_ids = lax.broadcasted_iota(jnp.int32, (GROUP, LANES), 0)
    carry = jnp.zeros((n, 1), F32)
    label_sum = jnp.zeros((2 * n, GROUP), F32)
    offset = my_place * deep
    for g in range(lane_groups):
        cols = slice(g * LANES, (g + 1) * LANES)
        named = target_ref[:, cols]
        match = jnp.where(device_ids == named, 1.0, 0.0)
        local = dot(match.astype(BF16), upper)
        rank = jnp.sum(match * (local + carry), axis=0, keepdims=True) - 1.0
        carry = carry + local[:, LANES - 1 :]
        rank = rank.astype(jnp.int32)
        slot = jnp.where(rank < deep, rank, rank - deep + LANES)
        row = named * deep
        place = (row & (LANES - 1)) + 2 * (row - (row & (LANES - 1))) + slot
        pos_ref[:, cols] = place
        posb_ref[cols, :] = jnp.broadcast_to(place.astype(F32), (LANES, LANES)).T
        mark = label_ref[:, cols] + 1
        high = match * (mark >> 5).astype(F32)
        low = match * (mark & 31).astype(F32)
        label_sum = label_sum + lax.dot_general(
            jnp.concatenate([high, low], axis=0).astype(BF16),
            hot(slot_ids == slot + offset),
            (((1,), (1,)), ((), ())),
            preferred_element_type=F32,
        )
    labels = 32.0 * label_sum[:n] + label_sum[n:]
    for t in range(n):
        lab_out[t] = labels[t : t + 1]

    pl.semaphore_wait(barrier, n - 1)

    lab_in[me] = lab_out[me]
    for step in range(1, n):
        t = lax.rem(me + step, n)
        pltpu.make_async_remote_copy(
            src_ref=lab_out.at[t],
            dst_ref=lab_in.at[me],
            send_sem=lab_send,
            recv_sem=lab_recv,
            device_id=device(t),
            device_id_type=MESH,
        ).start()

    lane = lax.broadcasted_iota(jnp.int32, (1, LANES), 1)
    left_lanes = lane < LANES // 2

    def split(values):
        other = pltpu.roll(values, LANES // 2, 1)
        return (
            (jnp.where(left_lanes, values, 0.0), jnp.where(left_lanes, other, 0.0)),
            (jnp.where(left_lanes, 0.0, other), jnp.where(left_lanes, 0.0, values)),
        )

    node_ids = lax.broadcasted_iota(jnp.int32, (NODE_BLOCK, LANES), 0)

    def find_terms(half):
        def terms_of(g, _):
            cols = pl.ds(pl.multiple_of(g * LANES, LANES), LANES)

            def chunk(k, sums):
                rows = pl.ds(pl.multiple_of(k * 8, 8), 8)
                residual = resid_ref[rows, cols]
                halved = 0.5 * residual
                vectors = [
                    tangent_ref[c, rows, cols] * halved for c in range(2 * half, min(3, 2 * half + 2))
                ]
                tails = ends_ref[0, rows, cols]
                heads = ends_ref[1, rows, cols]
                sums = list(sums)
                for e in range(8):
                    at_tail = node_ids == tails[e : e + 1]
                    at_head = node_ids == heads[e : e + 1]
                    either = at_tail | at_head
                    for c, vector in enumerate(vectors):
                        sums[c] = sums[c] + jnp.where(either, vector[e : e + 1], 0.0)
                    if half:
                        value = residual[e : e + 1]
                        sums[1] = sums[1] + jnp.where(
                            at_head, value, jnp.where(at_tail, -value, 0.0)
                        )
                return tuple(sums)

            zero = jnp.zeros((NODE_BLOCK, LANES), F32)
            sums = lax.fori_loop(0, BLOCK_EDGES // 8, chunk, (zero,) * 2)
            turned = jnp.concatenate(list(sums) + [zero, zero], axis=0).T
            for side, values in enumerate((turned, pltpu.roll(turned, LANES // 2, 1))):
                at = pl.ds(pl.multiple_of(side * blocks + g * LANES, LANES), LANES)
                high, low = halves(values)
                rows_ref[half, at, :LANES] = high
                rows_ref[half, at, LANES:] = low
            return 0

        lax.fori_loop(0, lane_groups, terms_of, 0)

    def rows_copy(src, dst, sends, recvs, half, step, turn):
        t = partner(to_group(step), turn)
        return pltpu.make_async_remote_copy(
            src_ref=src.at[half, pl.ds(pl.multiple_of(t * deep, deep), deep)],
            dst_ref=dst.at[half, pl.ds(pl.multiple_of(me * deep, deep), deep)],
            send_sem=sends.at[half, step],
            recv_sem=recvs.at[half, step],
            device_id=device(t),
            device_id_type=MESH,
        )

    def group_copy(src, dst, sends, recvs, half, step):
        size = LANES if step else LANES - deep
        return pltpu.make_async_remote_copy(
            src_ref=src.at[half, pl.ds(0, size)],
            dst_ref=dst.at[half, pl.ds(0, size)],
            send_sem=sends.at[half, step],
            recv_sem=recvs.at[half, step],
            device_id=device(me),
            device_id_type=MESH,
        )

    def send_group(src, dst, sends, recvs, half, step):
        for turn in range(peers):
            if step == 0 and turn == 0:
                mine = pl.ds(pl.multiple_of(me * deep, deep), deep)
                dst[half, mine, :] = src[half, mine, :]
            else:
                rows_copy(src, dst, sends, recvs, half, step, turn).start()

    row_ids = lax.broadcasted_iota(jnp.int32, (LANES, blocks), 0)

    def send_terms(half):
        for step in order:
            group = to_group(step)
            places = pos_ref[...] - group * GROUP
            chosen = jnp.concatenate(
                [hot(places == row_ids), hot(places == row_ids + LANES)], axis=1
            )
            at = pl.ds(pl.multiple_of(group * LANES, LANES), LANES)
            send_ref[half, at, :] = folded(dot(chosen, rows_ref[half]))
            send_group(send_ref, got_ref, go_send, go_recv, half, step)

    def label_row(group):
        total = lab_in[group * peers]
        for k in range(1, peers):
            total = total + lab_in[group * peers + k]
        return total

    def take_labels():
        pltpu.make_async_remote_copy(
            src_ref=lab_out.at[pl.ds(0, n - 1)],
            dst_ref=lab_in.at[pl.ds(0, n - 1)],
            send_sem=lab_send,
            recv_sem=lab_recv,
            device_id=device(me),
            device_id_type=MESH,
        ).wait()
        for g in range(groups):
            row = label_row(g)
            for k in range(2):
                at = slice(g * GROUP + k * LANES, g * GROUP + (k + 1) * LANES)
                labb_ref[at, :] = jnp.broadcast_to(
                    row[:, k * LANES : (k + 1) * LANES], (LANES, LANES)
                ).T

    def block_ids(side):
        rows = lax.broadcasted_iota(jnp.int32, (slab, LANES), 0)
        return jnp.concatenate(
            [(rows + (2 * s + side) * slab + 1).astype(F32) for s in range(slices)], axis=0
        )

    def sum_terms(half):
        for k, step in enumerate(order):
            group_copy(send_ref, got_ref, go_send, go_recv, half, step).wait_recv()
            source = from_group(step)
            marks = label_row(source)
            chosen = jnp.concatenate(
                [
                    hot(block_ids(side) == marks[:, part * LANES : (part + 1) * LANES])
                    for side in range(2)
                    for part in range(2)
                ],
                axis=1,
            )
            got = got_ref[half, pl.ds(pl.multiple_of(source * LANES, LANES), LANES), :]
            placed = split(got)
            high, low = halves(jnp.concatenate(placed[0] + placed[1], axis=0))
            part = folded(dot(chosen, jnp.concatenate([high, low], axis=1)))
            acc_ref[half] = part if k == 0 else acc_ref[half] + part

    inner = lax.broadcasted_iota(jnp.int32, (slab, LANES), 0) & 7
    node = lax.broadcasted_iota(jnp.int32, (slab, LANES), 1) & (NODE_BLOCK - 1)
    last_node = node == NODE_BLOCK - 1
    first_node = node == 0
    last_inner = inner == 7
    first_inner = inner == 0
    left = lax.rem(me + n - 1, n)
    right = lax.rem(me + 1, n)

    def own(s):
        return slice(s * slab, (s + 1) * slab)

    def stored(s):
        return slice((s + 1) * slab, (s + 2) * slab)

    def halo(half, level, side):
        at = stored(0) if side == 0 else stored(slices - 1)
        to = stored(slices) if side == 0 else own(0)
        return pltpu.make_async_remote_copy(
            src_ref=field_ref.at[half, level, at],
            dst_ref=field_ref.at[half, level, to],
            send_sem=halo_send.at[half, level, side],
            recv_sem=halo_recv.at[half, level, side],
            device_id=device(left if side == 0 else right),
            device_id_type=MESH,
        )

    def smooth(half):
        scale = jnp.where((lane & (LANES // 2 - 1)) < NODE_BLOCK, 1.0, 0.5 if half else 1.0)
        scale = scale.astype(F32)
        top = 12.0 + 8.0 * scale
        bottom = top / 8.0
        centre = (top + bottom) / 2.0
        radius = (top - bottom) / 2.0
        ratio = centre / radius
        first = 1.0 / ratio
        second = 1.0 / (2.0 * ratio - first)
        coef_one = second * first
        coef_two = 2.0 * second / radius
        inverse = 1.0 / centre

        def applied(level, s):
            field = field_ref.at[half, level]
            here = field[stored(s)]
            beside = field[own(s)] + field[stored(s + 1)]
            inward = jnp.where(left_lanes, 0.0, pltpu.roll(here[-8:], LANES // 2, 1))
            outward = jnp.where(left_lanes, pltpu.roll(here[:8], LANES // 2, 1), 0.0)
            beside = beside + jnp.concatenate([inward, here[:-8]], axis=0)
            beside = beside + jnp.concatenate([here[8:], outward], axis=0)
            after = pltpu.roll(pltpu.roll(here, slab - 1, 0), NODE_BLOCK - 1, 1)
            after = jnp.where(last_inner, 0.0, after)
            before = pltpu.roll(pltpu.roll(here, 1, 0), LANES - NODE_BLOCK + 1, 1)
            before = jnp.where(first_inner, 0.0, before)
            beside = beside + jnp.where(last_node, after, pltpu.roll(here, LANES - 1, 1))
            beside = beside + jnp.where(first_node, before, pltpu.roll(here, 1, 1))
            return diag_ref[half, own(s)] * here - beside

        def stage(level, body):
            if level:
                for side in range(2):
                    halo(half, level - 1, side).wait_recv()
            for s in (0, slices - 1):
                body(s)
            if level < 3:
                for side in range(2):
                    halo(half, level, side).start()
            for s in range(1, slices - 1):
                body(s)

        def begin(s):
            field_ref[half, 0, stored(s)] = acc_ref[half, own(s)] * inverse

        def sweep(s):
            rest = acc_ref[half, own(s)] - applied(0, s)
            step = field_ref[half, 0, stored(s)]
            field_ref[half, 1, stored(s)] = step + (coef_one * step + coef_two * rest)

        def residue(s):
            rest = acc_ref[half, own(s)] - applied(1, s)
            rest_ref[half, own(s)] = rest
            field_ref[half, 2, stored(s)] = rest * inverse

        def finish(s):
            step = field_ref[half, 2, stored(s)]
            rest = rest_ref[half, own(s)] - applied(2, s)
            total = (field_ref[half, 1, stored(s)] + step) + (coef_one * step + coef_two * rest)
            placed = split(total)
            for part in range(2):
                for side in range(2):
                    start = (2 * part + side) * nodal + s * slab
                    high, low = halves(placed[part][side])
                    sol_ref[half, start : start + slab, :LANES] = high
                    sol_ref[half, start : start + slab, LANES:] = low

        for level, body in enumerate((begin, sweep, residue, finish)):
            stage(level, body)

    lane_ids = lax.broadcasted_iota(jnp.int32, (LANES, LANES), 1).astype(F32)

    def send_back(half):
        for step in order:
            group = to_group(step)
            chosen = []
            for part in range(2):
                start = pl.multiple_of(group * GROUP + part * LANES, LANES)
                marks = labb_ref[pl.ds(start, LANES), :] - 1.0
                for side in range(2):
                    for s in range(slices):
                        chosen.append(hot(marks == lane_ids + float((2 * s + side) * slab)))
            at = pl.ds(pl.multiple_of(group * LANES, LANES), LANES)
            back_ref[half, at, :] = folded(dot(jnp.concatenate(chosen, axis=1), sol_ref[half]))
            send_group(back_ref, ret_ref, back_send, back_recv, half, step)

    slot_lanes = lax.broadcasted_iota(jnp.int32, (blocks, LANES), 1).astype(F32)

    def take_back(half):
        for k, step in enumerate(order):
            group_copy(back_ref, ret_ref, back_send, back_recv, half, step).wait_recv()
            source = from_group(step)
            places = posb_ref[...] - (source * GROUP).astype(F32)
            chosen = jnp.concatenate(
                [hot(places == slot_lanes), hot(places == slot_lanes + float(LANES))], axis=1
            )
            got = ret_ref[half, pl.ds(pl.multiple_of(source * LANES, LANES), LANES), :]
            high = got.astype(BF16).astype(F32)
            low = got - high
            turn = LANES // 2
            pieces = [
                jnp.where(left_lanes, high, pltpu.roll(low, turn, 1)),
                jnp.where(left_lanes, pltpu.roll(high, turn, 1), low),
            ]
            part = dot(chosen, jnp.concatenate(pieces, axis=0).astype(BF16))
            mine_ref[...] = part if k == 0 else mine_ref[...] + part

    def lift(half):
        def lift_group(g, _):
            cols = pl.ds(pl.multiple_of(g * LANES, LANES), LANES)
            values = mine_ref[cols, :].T
            values = values[: LANES // 2] + values[LANES // 2 :]

            for k in range(BLOCK_EDGES // 8):
                rows = slice(k * 8, k * 8 + 8)

                def taken(c, ids, part):
                    found = None
                    for piece in range(NODE_BLOCK // 8):
                        start = c * NODE_BLOCK + piece * 8
                        here = jnp.take_along_axis(
                            values[start : start + 8], ids, axis=0, mode="promise_in_bounds"
                        )
                        found = here if piece == 0 else jnp.where(part == piece, here, found)
                    return found

                tails = ends_ref[0, rows, cols]
                heads = ends_ref[1, rows, cols]
                tail_at, tail_part = tails & 7, tails >> 3
                head_at, head_part = heads & 7, heads >> 3
                pair = taken(0, head_at, head_part) + taken(0, tail_at, tail_part)
                total = tangent_ref[2 * half, rows, cols] * pair
                if half:
                    drop = taken(1, head_at, head_part) - taken(1, tail_at, tail_part)
                    out_ref[rows, cols] = out_ref[rows, cols] + 0.5 * total + drop
                else:
                    pair = taken(1, head_at, head_part) + taken(1, tail_at, tail_part)
                    total = total + tangent_ref[1, rows, cols] * pair
                    out_ref[rows, cols] = (
                        jacobi_ref[rows, cols] * resid_ref[rows, cols] + 0.5 * total
                    )
            return 0

        lax.fori_loop(0, lane_groups, lift_group, 0)

    for half in range(2):
        find_terms(half)
        send_terms(half)
    take_labels()
    for half in range(2):
        sum_terms(half)
        smooth(half)
        send_back(half)
    for half in range(2):
        take_back(half)
        lift(half)

    for half in range(2):
        for step in order:
            group_copy(send_ref, got_ref, go_send, go_recv, half, step).wait_send()
            group_copy(back_ref, ret_ref, back_send, back_recv, half, step).wait_send()
        for level in range(3):
            for side in range(2):
                halo(half, level, side).wait_send()


def per_device(n, n_node, residual, tangent, jacobi, ends, target, node_block, sigma):
    blocks = residual.shape[1]
    slices, rows_radial, rows_axial = sigma.shape
    nodal = slices * rows_radial * rows_axial // NODE_BLOCK // 2
    slots = 2 * blocks
    rows = slots // 2
    parts = sigma.reshape(slices, 2, LANES, NODE_BLOCK)
    inner, outer = (parts[:, k].reshape(nodal, NODE_BLOCK) for k in range(2))
    diag = 6.0 + jnp.stack(
        [
            jnp.concatenate([inner, inner, outer, outer], axis=1),
            jnp.concatenate([inner, 0.5 * inner, outer, 0.5 * outer], axis=1),
        ]
    )
    groups = slots // GROUP
    vmem = pl.BlockSpec(memory_space=pltpu.VMEM)
    return pl.pallas_call(
        functools.partial(kernel, n, n_node, slices),
        out_shape=jax.ShapeDtypeStruct(residual.shape, F32),
        in_specs=[vmem] * 7,
        out_specs=vmem,
        scratch_shapes=[
            pltpu.VMEM((1, blocks), jnp.int32),
            pltpu.VMEM((blocks, LANES), F32),
            pltpu.VMEM((n, 1, GROUP), F32),
            pltpu.VMEM((n, 1, GROUP), F32),
            pltpu.VMEM((slots, LANES), F32),
            pltpu.VMEM((2, 2 * blocks, 2 * LANES), BF16),
            pltpu.VMEM((2, rows, LANES), F32),
            pltpu.VMEM((2, rows, LANES), F32),
            pltpu.VMEM((2, nodal, LANES), F32),
            pltpu.VMEM((2, nodal, LANES), F32),
            pltpu.VMEM((2, 3, nodal + 2 * LANES, LANES), F32),
            pltpu.VMEM((2, 4 * nodal, 2 * LANES), BF16),
            pltpu.VMEM((2, rows, LANES), F32),
            pltpu.VMEM((2, rows, LANES), F32),
            pltpu.VMEM((blocks, LANES), F32),
            pltpu.SemaphoreType.DMA,
            pltpu.SemaphoreType.DMA,
            pltpu.SemaphoreType.DMA((2, groups)),
            pltpu.SemaphoreType.DMA((2, groups)),
            pltpu.SemaphoreType.DMA((2, groups)),
            pltpu.SemaphoreType.DMA((2, groups)),
            pltpu.SemaphoreType.DMA((2, 3, 2)),
            pltpu.SemaphoreType.DMA((2, 3, 2)),
        ],
        compiler_params=pltpu.CompilerParams(
            collective_id=0, has_side_effects=True, vmem_limit_bytes=48 * 1024 * 1024
        ),
    )(
        residual,
        tangent,
        jacobi,
        ends,
        target.reshape(1, blocks),
        node_block.reshape(1, blocks),
        diag,
    )


def solution(mesh):
    in_specs = (
        P(None, ("edge", "node")),
        P(None, None, ("edge", "node")),
        P(None, ("edge", "node")),
        P(None, None, ("edge", "node")),
        P(("edge", "node"), None),
        P(("edge", "node")),
        P(("edge", "node"), None, None),
    )
    out_specs = P(None, ("edge", "node"))
    n_node = mesh.shape["node"]
    n = mesh.shape["edge"] * n_node
    return jax.shard_map(
        functools.partial(per_device, n, n_node),
        mesh=mesh,
        in_specs=in_specs,
        out_specs=out_specs,
        check_vma=False,
    )
```

time: 81.1 us -> 82.2 us (1.014)
  no operation moved by 1% of the time
where the time goes in v2:
time: 82.2 us; the launch traced here: 82.1 us
  Pallas kernels  78.5 us (95%)
  local copies, waits for them, and re-layouts  3.01 us (4%)
    pallas_call x1, Pallas kernels, per_device(): pl.pallas_call(functools.partial(kernel, n, n_node, slices), out_shape=ja...  78.5 us
    unnamed x13, local copies, waits for them, and re-layouts  1.91 us

profile of v2, /device:TPU:0, one launch (start us, length us, event | category | flops | bytes accessed | tf_op | source)
XLA Modules:
  0.0 82.1 jit_solution(2192872737505088194)
XLA Ops:
  0.0 1.1 %reshape.11 = f32[4,2,128,32]{3,2,1,0:T(8,128)S(1)} reshape(f32[4,32,256]{2,1,0:T(8,128)} %param.13) | data formatting | bytes 262144 | tf_op jit(solution)/shard_map/reshape | solution.py:499
  1.2 0.0 copy-start.1
  1.2 0.0 copy-start.3
  1.2 0.0 copy-start.4
  1.2 0.0 copy-start.5
  1.2 0.4 maximum_bitcast_fusion
  1.6 0.0 copy-start
  1.6 0.0 copy-start.2
  1.7 0.5 copy-done.1
  2.2 0.1 copy-done.3
  2.3 0.0 copy-done.4
  2.3 0.0 copy-done.5
  2.3 0.5 copy-done
  2.8 0.1 copy-done.2
  2.9 78.5 %shard_map.73 = f32[64,1024]{1,0:T(8,128)S(1)} custom-call(f32[64,1024]{1,0:T(8,128)S(1)} %copy-done.2, f32[3,64,1024]{2,1,0:T(8,128)S(1)} %copy-done, f32[64,1024]{1,0:T(8,128)S(1)} %copy-done.3, s32[2,64,1024]{2,1,0:T(8,128)S(1)} %copy-done.1, s32[1,1024]{1,0:T(1,128)S(1)} %bitcast.10, s32[1,1024]{1,0:T(1,128)S(1)} %bitcast.11, ...), custom_call_target="tpu_custom_call" | custom-call | tf_op jit(solution)/shard_map/pallas_call | solution.py:509
  81.4 0.7 copy.11
  (3 shorter events, 0.1 us)
Async XLA Ops:
  1.2 1.0 %copy-start.1 = (s32[2,64,1024]{2,1,0:T(8,128)S(1)}, s32[2,64,1024]{2,1,0:T(8,128)}, u32[]{:S(2)}) copy-start(s32[2,64,1024]{2,1,0:T(8,128)} %ends_ref.1) | copy-start | bytes 1572868
  1.2 1.1 %copy-start.3 = (f32[64,1024]{1,0:T(8,128)S(1)}, f32[64,1024]{1,0:T(8,128)}, u32[]{:S(2)}) copy-start(f32[64,1024]{1,0:T(8,128)} %jacobi_ref.1) | copy-start | bytes 786436
  1.2 1.1 %copy-start.4 = (s32[1024,1]{0,1:T(1,128)S(1)}, s32[1024,1]{0,1:T(1,128)}, u32[]{:S(2)}) copy-start(s32[1024,1]{0,1:T(1,128)} %param.11) | copy-start | bytes 12292
  1.2 1.1 %copy-start.5 = (s32[1024]{0:T(1024)S(1)}, s32[1024]{0:T(1024)}, u32[]{:S(2)}) copy-start(s32[1024]{0:T(1024)} %param.12) | copy-start | bytes 12292
  1.6 1.2 %copy-start = (f32[3,64,1024]{2,1,0:T(8,128)S(1)}, f32[3,64,1024]{2,1,0:T(8,128)}, u32[]{:S(2)}) copy-start(f32[3,64,1024]{2,1,0:T(8,128)} %tangent_ref.1) | copy-start | bytes 2359300
  1.6 1.2 %copy-start.2 = (f32[64,1024]{1,0:T(8,128)S(1)}, f32[64,1024]{1,0:T(8,128)}, u32[]{:S(2)}) copy-start(f32[64,1024]{1,0:T(8,128)} %resid_ref.1) | copy-start | bytes 786436

commit v3 on v2

--- a/solution.py
+++ b/solution.py
@@ -17,12 +17,6 @@
 MESH = pl.DeviceIdType.MESH
 
 
-def halves(values):
-    high = values.astype(BF16)
-    low = (values - high.astype(F32)).astype(BF16)
-    return high, low
-
-
 def hot(mask):
     return jnp.where(mask, 1.0, 0.0).astype(BF16)
 
@@ -31,8 +25,23 @@
     return jnp.dot(a, b, preferred_element_type=F32)
 
 
+def left_lanes():
+    return lax.broadcasted_iota(jnp.int32, (1, LANES), 1) < LANES // 2
+
+
+def pieces(values):
+    high = values.astype(BF16).astype(F32)
+    low = values - high
+    turn = LANES // 2
+    upper = jnp.where(left_lanes(), high, pltpu.roll(low, turn, 1))
+    lower = jnp.where(left_lanes(), pltpu.roll(high, turn, 1), low)
+    return jnp.concatenate([upper, lower], axis=0).astype(BF16)
+
+
 def folded(product):
-    return product[:, :LANES] + product[:, LANES:]
+    both = product + pltpu.roll(product, LANES // 2, 1)
+    rows = product.shape[0] // 2
+    return jnp.where(left_lanes(), both[:rows], both[rows:])
 
 
 def order_of(groups):
@@ -49,19 +58,24 @@
     ends_ref,
     target_ref,
     label_ref,
-    diag_ref,
+    sigma_ref,
     out_ref,
     pos_ref,
     posb_ref,
     lab_out,
     lab_in,
-    labb_ref,
+    to_slot_ref,
+    to_node_ref,
+    from_node_ref,
+    from_slot_ref,
     rows_ref,
     send_ref,
     got_ref,
     acc_ref,
+    source_ref,
+    wide_sigma_ref,
+    first_ref,
     rest_ref,
-    field_ref,
     sol_ref,
     back_ref,
     ret_ref,
@@ -74,6 +88,8 @@
     back_recv,
     halo_send,
     halo_recv,
+    sigma_send,
+    sigma_recv,
 ):
     me = lax.axis_index("edge") * n_node + lax.axis_index("node")
     blocks = resid_ref.shape[1]
@@ -141,29 +157,18 @@
     for t in range(n):
         lab_out[t] = labels[t : t + 1]
 
-    pl.semaphore_wait(barrier, n - 1)
-
-    lab_in[me] = lab_out[me]
-    for step in range(1, n):
-        t = lax.rem(me + step, n)
-        pltpu.make_async_remote_copy(
-            src_ref=lab_out.at[t],
-            dst_ref=lab_in.at[me],
-            send_sem=lab_send,
-            recv_sem=lab_recv,
-            device_id=device(t),
-            device_id_type=MESH,
-        ).start()
-
-    lane = lax.broadcasted_iota(jnp.int32, (1, LANES), 1)
-    left_lanes = lane < LANES // 2
-
-    def split(values):
-        other = pltpu.roll(values, LANES // 2, 1)
-        return (
-            (jnp.where(left_lanes, values, 0.0), jnp.where(left_lanes, other, 0.0)),
-            (jnp.where(left_lanes, 0.0, other), jnp.where(left_lanes, 0.0, values)),
-        )
+    def send_labels():
+        lab_in[me] = lab_out[me]
+        for step in range(1, n):
+            t = lax.rem(me + step, n)
+            pltpu.make_async_remote_copy(
+                src_ref=lab_out.at[t],
+                dst_ref=lab_in.at[me],
+                send_sem=lab_send,
+                recv_sem=lab_recv,
+                device_id=device(t),
+                device_id_type=MESH,
+            ).start()
 
     node_ids = lax.broadcasted_iota(jnp.int32, (NODE_BLOCK, LANES), 0)
 
@@ -196,12 +201,9 @@
 
             zero = jnp.zeros((NODE_BLOCK, LANES), F32)
             sums = lax.fori_loop(0, BLOCK_EDGES // 8, chunk, (zero,) * 2)
-            turned = jnp.concatenate(list(sums) + [zero, zero], axis=0).T
-            for side, values in enumerate((turned, pltpu.roll(turned, LANES // 2, 1))):
-                at = pl.ds(pl.multiple_of(side * blocks + g * LANES, LANES), LANES)
-                high, low = halves(values)
-                rows_ref[half, at, :LANES] = high
-                rows_ref[half, at, LANES:] = low
+            high = [total.astype(BF16).astype(F32) for total in sums]
+            low = [total - part for total, part in zip(sums, high)]
+            rows_ref[half, cols, :] = jnp.concatenate(high + low, axis=0).T.astype(BF16)
             return 0
 
         lax.fori_loop(0, lane_groups, terms_of, 0)
@@ -236,18 +238,29 @@
             else:
                 rows_copy(src, dst, sends, recvs, half, step, turn).start()
 
-    row_ids = lax.broadcasted_iota(jnp.int32, (LANES, blocks), 0)
+    row_ids = lax.broadcasted_iota(jnp.int32, (GROUP, blocks), 0)
 
     def send_terms(half):
         for step in order:
             group = to_group(step)
-            places = pos_ref[...] - group * GROUP
-            chosen = jnp.concatenate(
-                [hot(places == row_ids), hot(places == row_ids + LANES)], axis=1
-            )
-            at = pl.ds(pl.multiple_of(group * LANES, LANES), LANES)
-            send_ref[half, at, :] = folded(dot(chosen, rows_ref[half]))
+            at = pl.ds(pl.multiple_of(group * GROUP, GROUP), GROUP)
+            if half == 0:
+                chosen = hot(pos_ref[...] - group * GROUP == row_ids)
+                to_slot_ref[at, :] = chosen
+            else:
+                chosen = to_slot_ref[at, :]
+            rows = pl.ds(pl.multiple_of(group * LANES, LANES), LANES)
+            send_ref[half, rows, :] = folded(dot(chosen, rows_ref[half]))
             send_group(send_ref, got_ref, go_send, go_recv, half, step)
+
+    slot_lanes = lax.broadcasted_iota(jnp.int32, (blocks, LANES), 1).astype(F32)
+
+    def prepare_return():
+        for g in range(groups):
+            for part in range(2):
+                lanes = slice(part * LANES, (part + 1) * LANES)
+                ids = slot_lanes + float(g * GROUP + part * LANES)
+                from_slot_ref[g, :, lanes] = hot(posb_ref[...] == ids)
 
     def label_row(group):
         total = lab_in[group * peers]
@@ -266,11 +279,24 @@
         ).wait()
         for g in range(groups):
             row = label_row(g)
-            for k in range(2):
-                at = slice(g * GROUP + k * LANES, g * GROUP + (k + 1) * LANES)
-                labb_ref[at, :] = jnp.broadcast_to(
-                    row[:, k * LANES : (k + 1) * LANES], (LANES, LANES)
-                ).T
+            for part in range(2):
+                lanes = slice(part * LANES, (part + 1) * LANES)
+                marks = row[:, lanes]
+                for side in range(2):
+                    rows = slice(side * nodal, (side + 1) * nodal)
+                    to_node_ref[g, rows, lanes] = hot(block_ids(side) == marks)
+        for g in range(groups):
+            row = label_row(g)
+            for part in range(2):
+                start = g * GROUP + part * LANES
+                marks = row[:, part * LANES : (part + 1) * LANES]
+                marks = jnp.broadcast_to(marks, (LANES, LANES)).T
+                for side in range(2):
+                    for s in range(slices):
+                        column = side * nodal + s * slab
+                        from_node_ref[start : start + LANES, column : column + slab] = hot(
+                            marks == lane_ids + float((2 * s + side) * slab + 1)
+                        )
 
     def block_ids(side):
         rows = lax.broadcasted_iota(jnp.int32, (slab, LANES), 0)
@@ -278,24 +304,16 @@
             [(rows + (2 * s + side) * slab + 1).astype(F32) for s in range(slices)], axis=0
         )
 
+    lane_ids = lax.broadcasted_iota(jnp.int32, (LANES, LANES), 1).astype(F32)
+
     def sum_terms(half):
         for k, step in enumerate(order):
             group_copy(send_ref, got_ref, go_send, go_recv, half, step).wait_recv()
             source = from_group(step)
-            marks = label_row(source)
-            chosen = jnp.concatenate(
-                [
-                    hot(block_ids(side) == marks[:, part * LANES : (part + 1) * LANES])
-                    for side in range(2)
-                    for part in range(2)
-                ],
-                axis=1,
-            )
             got = got_ref[half, pl.ds(pl.multiple_of(source * LANES, LANES), LANES), :]
-            placed = split(got)
-            high, low = halves(jnp.concatenate(placed[0] + placed[1], axis=0))
-            part = folded(dot(chosen, jnp.concatenate([high, low], axis=1)))
-            acc_ref[half] = part if k == 0 else acc_ref[half] + part
+            part = dot(to_node_ref[source], pieces(got))
+            acc_ref[...] = part if k == 0 else acc_ref[...] + part
+        source_ref[half, at_slices(0, slices, 3)] = folded(acc_ref[...])
 
     inner = lax.broadcasted_iota(jnp.int32, (slab, LANES), 0) & 7
     node = lax.broadcasted_iota(jnp.int32, (slab, LANES), 1) & (NODE_BLOCK - 1)
@@ -306,25 +324,35 @@
     left = lax.rem(me + n - 1, n)
     right = lax.rem(me + 1, n)
 
-    def own(s):
-        return slice(s * slab, (s + 1) * slab)
-
-    def stored(s):
-        return slice((s + 1) * slab, (s + 2) * slab)
-
-    def halo(half, level, side):
-        at = stored(0) if side == 0 else stored(slices - 1)
-        to = stored(slices) if side == 0 else own(0)
+    def at_slices(first, last, margin):
+        return slice((first + margin) * slab, (last + margin) * slab)
+
+    def halo(half, side):
+        at = at_slices(0, 3, 3) if side == 0 else at_slices(slices - 3, slices, 3)
+        to = at_slices(slices, slices + 3, 3) if side == 0 else at_slices(-3, 0, 3)
         return pltpu.make_async_remote_copy(
-            src_ref=field_ref.at[half, level, at],
-            dst_ref=field_ref.at[half, level, to],
-            send_sem=halo_send.at[half, level, side],
-            recv_sem=halo_recv.at[half, level, side],
+            src_ref=source_ref.at[half, at],
+            dst_ref=source_ref.at[half, to],
+            send_sem=halo_send.at[half, side],
+            recv_sem=halo_recv.at[half, side],
             device_id=device(left if side == 0 else right),
             device_id_type=MESH,
         )
 
+    def sigma_halo(side):
+        at = at_slices(0, 2, 2) if side == 0 else at_slices(slices - 2, slices, 2)
+        to = at_slices(slices, slices + 2, 2) if side == 0 else at_slices(-2, 0, 2)
+        return pltpu.make_async_remote_copy(
+            src_ref=wide_sigma_ref.at[at],
+            dst_ref=wide_sigma_ref.at[to],
+            send_sem=sigma_send.at[side],
+            recv_sem=sigma_recv.at[side],
+            device_id=device(left if side == 0 else right),
+            device_id_type=MESH,
+        )
+
     def smooth(half):
+        lane = lax.broadcasted_iota(jnp.int32, (1, LANES), 1)
         scale = jnp.where((lane & (LANES // 2 - 1)) < NODE_BLOCK, 1.0, 0.5 if half else 1.0)
         scale = scale.astype(F32)
         top = 12.0 + 8.0 * scale
@@ -337,13 +365,14 @@
         coef_one = second * first
         coef_two = 2.0 * second / radius
         inverse = 1.0 / centre
-
-        def applied(level, s):
-            field = field_ref.at[half, level]
-            here = field[stored(s)]
-            beside = field[own(s)] + field[stored(s + 1)]
-            inward = jnp.where(left_lanes, 0.0, pltpu.roll(here[-8:], LANES // 2, 1))
-            outward = jnp.where(left_lanes, pltpu.roll(here[:8], LANES // 2, 1), 0.0)
+        source = source_ref.at[half]
+
+        def applied(field, margin, s):
+            here = field[at_slices(s, s + 1, margin)]
+            beside = field[at_slices(s - 1, s, margin)] + field[at_slices(s + 1, s + 2, margin)]
+            turn = LANES // 2
+            inward = jnp.where(left_lanes(), 0.0, pltpu.roll(here[-8:], turn, 1))
+            outward = jnp.where(left_lanes(), pltpu.roll(here[:8], turn, 1), 0.0)
             beside = beside + jnp.concatenate([inward, here[:-8]], axis=0)
             beside = beside + jnp.concatenate([here[8:], outward], axis=0)
             after = pltpu.roll(pltpu.roll(here, slab - 1, 0), NODE_BLOCK - 1, 1)
@@ -352,83 +381,60 @@
             before = jnp.where(first_inner, 0.0, before)
             beside = beside + jnp.where(last_node, after, pltpu.roll(here, LANES - 1, 1))
             beside = beside + jnp.where(first_node, before, pltpu.roll(here, 1, 1))
-            return diag_ref[half, own(s)] * here - beside
-
-        def stage(level, body):
-            if level:
-                for side in range(2):
-                    halo(half, level - 1, side).wait_recv()
-            for s in (0, slices - 1):
-                body(s)
-            if level < 3:
-                for side in range(2):
-                    halo(half, level, side).start()
-            for s in range(1, slices - 1):
-                body(s)
-
-        def begin(s):
-            field_ref[half, 0, stored(s)] = acc_ref[half, own(s)] * inverse
+            diag = 6.0 + scale * wide_sigma_ref[at_slices(s, s + 1, 2)]
+            return here, diag * here - beside
 
         def sweep(s):
-            rest = acc_ref[half, own(s)] - applied(0, s)
-            step = field_ref[half, 0, stored(s)]
-            field_ref[half, 1, stored(s)] = step + (coef_one * step + coef_two * rest)
+            here, image = applied(source, 3, s)
+            step = here * inverse
+            first_ref[at_slices(s, s + 1, 2)] = step + (
+                coef_one * step + coef_two * (here - image * inverse)
+            )
 
         def residue(s):
-            rest = acc_ref[half, own(s)] - applied(1, s)
-            rest_ref[half, own(s)] = rest
-            field_ref[half, 2, stored(s)] = rest * inverse
+            image = applied(first_ref, 2, s)[1]
+            rest_ref[at_slices(s, s + 1, 1)] = source[at_slices(s, s + 1, 3)] - image
 
         def finish(s):
-            step = field_ref[half, 2, stored(s)]
-            rest = rest_ref[half, own(s)] - applied(2, s)
-            total = (field_ref[half, 1, stored(s)] + step) + (coef_one * step + coef_two * rest)
-            placed = split(total)
-            for part in range(2):
-                for side in range(2):
-                    start = (2 * part + side) * nodal + s * slab
-                    high, low = halves(placed[part][side])
-                    sol_ref[half, start : start + slab, :LANES] = high
-                    sol_ref[half, start : start + slab, LANES:] = low
-
-        for level, body in enumerate((begin, sweep, residue, finish)):
-            stage(level, body)
-
-    lane_ids = lax.broadcasted_iota(jnp.int32, (LANES, LANES), 1).astype(F32)
+            here, image = applied(rest_ref, 1, s)
+            step = here * inverse
+            total = (first_ref[at_slices(s, s + 1, 2)] + step) + (
+                coef_one * step + coef_two * (here - image * inverse)
+            )
+            parts = pieces(total)
+            for side in range(2):
+                start = side * nodal + s * slab
+                sol_ref[half, start : start + slab, :] = parts[side * slab : (side + 1) * slab]
+
+        for side in range(2):
+            halo(half, side).start()
+        for s in range(1, slices - 1):
+            sweep(s)
+        for side in range(2):
+            halo(half, side).wait_recv()
+            if half == 0:
+                sigma_halo(side).wait_recv()
+        for s in [-2, -1, 0, slices - 1, slices, slices + 1]:
+            sweep(s)
+        for s in range(-1, slices + 1):
+            residue(s)
+        for s in range(slices):
+            finish(s)
 
     def send_back(half):
         for step in order:
             group = to_group(step)
-            chosen = []
-            for part in range(2):
-                start = pl.multiple_of(group * GROUP + part * LANES, LANES)
-                marks = labb_ref[pl.ds(start, LANES), :] - 1.0
-                for side in range(2):
-                    for s in range(slices):
-                        chosen.append(hot(marks == lane_ids + float((2 * s + side) * slab)))
-            at = pl.ds(pl.multiple_of(group * LANES, LANES), LANES)
-            back_ref[half, at, :] = folded(dot(jnp.concatenate(chosen, axis=1), sol_ref[half]))
+            chosen = from_node_ref[pl.ds(pl.multiple_of(group * GROUP, GROUP), GROUP), :]
+            rows = pl.ds(pl.multiple_of(group * LANES, LANES), LANES)
+            back_ref[half, rows, :] = folded(dot(chosen, sol_ref[half]))
             send_group(back_ref, ret_ref, back_send, back_recv, half, step)
-
-    slot_lanes = lax.broadcasted_iota(jnp.int32, (blocks, LANES), 1).astype(F32)
 
     def take_back(half):
         for k, step in enumerate(order):
             group_copy(back_ref, ret_ref, back_send, back_recv, half, step).wait_recv()
             source = from_group(step)
-            places = posb_ref[...] - (source * GROUP).astype(F32)
-            chosen = jnp.concatenate(
-                [hot(places == slot_lanes), hot(places == slot_lanes + float(LANES))], axis=1
-            )
             got = ret_ref[half, pl.ds(pl.multiple_of(source * LANES, LANES), LANES), :]
-            high = got.astype(BF16).astype(F32)
-            low = got - high
-            turn = LANES // 2
-            pieces = [
-                jnp.where(left_lanes, high, pltpu.roll(low, turn, 1)),
-                jnp.where(left_lanes, pltpu.roll(high, turn, 1), low),
-            ]
-            part = dot(chosen, jnp.concatenate(pieces, axis=0).astype(BF16))
+            part = dot(from_slot_ref[source], pieces(got))
             mine_ref[...] = part if k == 0 else mine_ref[...] + part
 
     def lift(half):
@@ -469,9 +475,16 @@
 
         lax.fori_loop(0, lane_groups, lift_group, 0)
 
-    for half in range(2):
-        find_terms(half)
-        send_terms(half)
+    wide_sigma_ref[at_slices(0, slices, 2)] = sigma_ref[...]
+    find_terms(0)
+    pl.semaphore_wait(barrier, n - 1)
+    send_labels()
+    send_terms(0)
+    for side in range(2):
+        sigma_halo(side).start()
+    find_terms(1)
+    send_terms(1)
+    prepare_return()
     take_labels()
     for half in range(2):
         sum_terms(half)
@@ -485,9 +498,10 @@
         for step in order:
             group_copy(send_ref, got_ref, go_send, go_recv, half, step).wait_send()
             group_copy(back_ref, ret_ref, back_send, back_recv, half, step).wait_send()
-        for level in range(3):
-            for side in range(2):
-                halo(half, level, side).wait_send()
+        for side in range(2):
+            halo(half, side).wait_send()
+    for side in range(2):
+        sigma_halo(side).wait_send()
 
 
 def per_device(n, n_node, residual, tangent, jacobi, ends, target, node_block, sigma):
@@ -498,12 +512,7 @@
     rows = slots // 2
     parts = sigma.reshape(slices, 2, LANES, NODE_BLOCK)
     inner, outer = (parts[:, k].reshape(nodal, NODE_BLOCK) for k in range(2))
-    diag = 6.0 + jnp.stack(
-        [
-            jnp.concatenate([inner, inner, outer, outer], axis=1),
-            jnp.concatenate([inner, 0.5 * inner, outer, 0.5 * outer], axis=1),
-        ]
-    )
+    cells = jnp.concatenate([inner, inner, outer, outer], axis=1)
     groups = slots // GROUP
     vmem = pl.BlockSpec(memory_space=pltpu.VMEM)
     return pl.pallas_call(
@@ -516,14 +525,19 @@
             pltpu.VMEM((blocks, LANES), F32),
             pltpu.VMEM((n, 1, GROUP), F32),
             pltpu.VMEM((n, 1, GROUP), F32),
-            pltpu.VMEM((slots, LANES), F32),
-            pltpu.VMEM((2, 2 * blocks, 2 * LANES), BF16),
+            pltpu.VMEM((slots, blocks), BF16),
+            pltpu.VMEM((groups, 2 * nodal, GROUP), BF16),
+            pltpu.VMEM((slots, 2 * nodal), BF16),
+            pltpu.VMEM((groups, blocks, GROUP), BF16),
+            pltpu.VMEM((2, blocks, LANES), BF16),
             pltpu.VMEM((2, rows, LANES), F32),
             pltpu.VMEM((2, rows, LANES), F32),
-            pltpu.VMEM((2, nodal, LANES), F32),
-            pltpu.VMEM((2, nodal, LANES), F32),
-            pltpu.VMEM((2, 3, nodal + 2 * LANES, LANES), F32),
-            pltpu.VMEM((2, 4 * nodal, 2 * LANES), BF16),
+            pltpu.VMEM((2 * nodal, LANES), F32),
+            pltpu.VMEM((2, nodal + 6 * LANES, LANES), F32),
+            pltpu.VMEM((nodal + 4 * LANES, LANES), F32),
+            pltpu.VMEM((nodal + 4 * LANES, LANES), F32),
+            pltpu.VMEM((nodal + 2 * LANES, LANES), F32),
+            pltpu.VMEM((2, 2 * nodal, LANES), BF16),
             pltpu.VMEM((2, rows, LANES), F32),
             pltpu.VMEM((2, rows, LANES), F32),
             pltpu.VMEM((blocks, LANES), F32),
@@ -533,8 +547,10 @@
             pltpu.SemaphoreType.DMA((2, groups)),
             pltpu.SemaphoreType.DMA((2, groups)),
             pltpu.SemaphoreType.DMA((2, groups)),
-            pltpu.SemaphoreType.DMA((2, 3, 2)),
-            pltpu.SemaphoreType.DMA((2, 3, 2)),
+            pltpu.SemaphoreType.DMA((2, 2)),
+            pltpu.SemaphoreType.DMA((2, 2)),
+            pltpu.SemaphoreType.DMA((2,)),
+            pltpu.SemaphoreType.DMA((2,)),
         ],
         compiler_params=pltpu.CompilerParams(
             collective_id=0, has_side_effects=True, vmem_limit_bytes=48 * 1024 * 1024
@@ -546,7 +562,7 @@
         ends,
         target.reshape(1, blocks),
         node_block.reshape(1, blocks),
-        diag,
+        cells,
     )
 
 

time: 82.2 us -> 75.3 us (0.916)
  the two profiles are of different devices: /device:TPU:0 before, /device:TPU:16 now
where the time goes in v3:
time: 75.3 us; the launch traced here: 75.2 us
  Pallas kernels  71.9 us (95%)
  local copies, waits for them, and re-layouts  2.9 us (4%)
    pallas_call x1, Pallas kernels, per_device(): pl.pallas_call(functools.partial(kernel, n, n_node, slices), out_shape=ja...  71.9 us
    unnamed x13, local copies, waits for them, and re-layouts  1.78 us

profile of v3, /device:TPU:16, one launch (start us, length us, event | category | flops | bytes accessed | tf_op | source)
XLA Modules:
  0.0 75.2 jit_solution(5785058531873571100)
XLA Ops:
  0.0 0.0 copy-start.5
  0.0 1.1 %reshape.11 = f32[4,2,128,32]{3,2,1,0:T(8,128)S(1)} reshape(f32[4,32,256]{2,1,0:T(8,128)} %param.13) | data formatting | bytes 262144 | tf_op jit(solution)/shard_map/reshape | solution.py:513
  1.1 0.0 copy-start
  1.1 0.0 copy-start.3
  1.2 0.0 copy-start.1
  1.2 0.0 copy-start.2
  1.2 0.0 copy-start.4
  1.2 0.3 pad_maximum_fusion.sigma_ref
  1.5 0.0 copy-done.5
  1.5 0.7 copy-done
  2.2 0.1 copy-done.3
  2.3 0.2 copy-done.1
  2.5 0.1 copy-done.2
  2.5 0.0 copy-done.4
  2.5 71.9 %shard_map.73 = f32[64,1024]{1,0:T(8,128)S(1)} custom-call(f32[64,1024]{1,0:T(8,128)S(1)} %copy-done.2, f32[3,64,1024]{2,1,0:T(8,128)S(1)} %copy-done, f32[64,1024]{1,0:T(8,128)S(1)} %copy-done.3, s32[2,64,1024]{2,1,0:T(8,128)S(1)} %copy-done.1, s32[1,1024]{1,0:T(1,128)S(1)} %bitcast.4, s32[1,1024]{1,0:T(1,128)S(1)} %bitcast.5, ...), custom_call_target="tpu_custom_call" | custom-call | tf_op jit(solution)/shard_map/pallas_call | solution.py:518
  74.5 0.7 copy.11
  (1 shorter events, 0.0 us)
Async XLA Ops:
  0.0 1.5 %copy-start.5 = (s32[1024]{0:T(1024)S(1)}, s32[1024]{0:T(1024)}, u32[]{:S(2)}) copy-start(s32[1024]{0:T(1024)} %param.12) | copy-start | bytes 12292
  1.1 1.1 %copy-start = (f32[3,64,1024]{2,1,0:T(8,128)S(1)}, f32[3,64,1024]{2,1,0:T(8,128)}, u32[]{:S(2)}) copy-start(f32[3,64,1024]{2,1,0:T(8,128)} %tangent_ref.1) | copy-start | bytes 2359300
  1.1 1.2 %copy-start.3 = (f32[64,1024]{1,0:T(8,128)S(1)}, f32[64,1024]{1,0:T(8,128)}, u32[]{:S(2)}) copy-start(f32[64,1024]{1,0:T(8,128)} %jacobi_ref.1) | copy-start | bytes 786436
  1.2 1.3 %copy-start.1 = (s32[2,64,1024]{2,1,0:T(8,128)S(1)}, s32[2,64,1024]{2,1,0:T(8,128)}, u32[]{:S(2)}) copy-start(s32[2,64,1024]{2,1,0:T(8,128)} %ends_ref.1) | copy-start | bytes 1572868
  1.2 1.4 %copy-start.2 = (f32[64,1024]{1,0:T(8,128)S(1)}, f32[64,1024]{1,0:T(8,128)}, u32[]{:S(2)}) copy-start(f32[64,1024]{1,0:T(8,128)} %resid_ref.1) | copy-start | bytes 786436
  1.2 1.3 %copy-start.4 = (s32[1024,1]{0,1:T(1,128)S(1)}, s32[1024,1]{0,1:T(1,128)}, u32[]{:S(2)}) copy-start(s32[1024,1]{0,1:T(1,128)} %param.11) | copy-start | bytes 12292

commit v4 on v3

--- a/solution.py
+++ b/solution.py
@@ -52,14 +52,17 @@
     n,
     n_node,
     slices,
-    resid_ref,
-    tangent_ref,
-    jacobi_ref,
-    ends_ref,
+    resid_in,
+    tangent_in,
+    ends_in,
     target_ref,
     label_ref,
     sigma_ref,
     out_ref,
+    resid_ref,
+    tangent_ref,
+    ends_ref,
+    load_sem,
     pos_ref,
     posb_ref,
     lab_out,
@@ -122,6 +125,15 @@
             barrier, inc=1, device_id=device(lax.rem(me + step, n)), device_id_type=MESH
         )
 
+    loads = [
+        pltpu.make_async_copy(src, dst, load_sem.at[k])
+        for k, (src, dst) in enumerate(
+            ((resid_in, resid_ref), (ends_in, ends_ref), (tangent_in, tangent_ref))
+        )
+    ]
+    for load in loads:
+        load.start()
+
     upper = hot(
         lax.broadcasted_iota(jnp.int32, (LANES, LANES), 0)
         <= lax.broadcasted_iota(jnp.int32, (LANES, LANES), 1)
@@ -240,8 +252,8 @@
 
     row_ids = lax.broadcasted_iota(jnp.int32, (GROUP, blocks), 0)
 
-    def send_terms(half):
-        for step in order:
+    def send_terms(half, steps):
+        for step in steps:
             group = to_group(step)
             at = pl.ds(pl.multiple_of(group * GROUP, GROUP), GROUP)
             if half == 0:
@@ -406,8 +418,6 @@
                 start = side * nodal + s * slab
                 sol_ref[half, start : start + slab, :] = parts[side * slab : (side + 1) * slab]
 
-        for side in range(2):
-            halo(half, side).start()
         for s in range(1, slices - 1):
             sweep(s)
         for side in range(2):
@@ -421,8 +431,8 @@
         for s in range(slices):
             finish(s)
 
-    def send_back(half):
-        for step in order:
+    def send_back(half, steps):
+        for step in steps:
             group = to_group(step)
             chosen = from_node_ref[pl.ds(pl.multiple_of(group * GROUP, GROUP), GROUP), :]
             rows = pl.ds(pl.multiple_of(group * LANES, LANES), LANES)
@@ -468,28 +478,36 @@
                 else:
                     pair = taken(1, head_at, head_part) + taken(1, tail_at, tail_part)
                     total = total + tangent_ref[1, rows, cols] * pair
-                    out_ref[rows, cols] = (
-                        jacobi_ref[rows, cols] * resid_ref[rows, cols] + 0.5 * total
-                    )
+                    out_ref[rows, cols] = 0.5 * total
             return 0
 
         lax.fori_loop(0, lane_groups, lift_group, 0)
 
     wide_sigma_ref[at_slices(0, slices, 2)] = sigma_ref[...]
+    for load in loads:
+        load.wait()
     find_terms(0)
     pl.semaphore_wait(barrier, n - 1)
     send_labels()
-    send_terms(0)
+    send_terms(0, order)
     for side in range(2):
         sigma_halo(side).start()
     find_terms(1)
-    send_terms(1)
+    send_terms(1, order[: groups // 2])
     prepare_return()
     take_labels()
-    for half in range(2):
-        sum_terms(half)
-        smooth(half)
-        send_back(half)
+    sum_terms(0)
+    for side in range(2):
+        halo(0, side).start()
+    send_terms(1, order[groups // 2 :])
+    smooth(0)
+    send_back(0, order[: groups // 2])
+    sum_terms(1)
+    for side in range(2):
+        halo(1, side).start()
+    send_back(0, order[groups // 2 :])
+    smooth(1)
+    send_back(1, order)
     for half in range(2):
         take_back(half)
         lift(half)
@@ -515,12 +533,17 @@
     cells = jnp.concatenate([inner, inner, outer, outer], axis=1)
     groups = slots // GROUP
     vmem = pl.BlockSpec(memory_space=pltpu.VMEM)
-    return pl.pallas_call(
+    hbm = pl.BlockSpec(memory_space=pl.ANY)
+    lifted = pl.pallas_call(
         functools.partial(kernel, n, n_node, slices),
         out_shape=jax.ShapeDtypeStruct(residual.shape, F32),
-        in_specs=[vmem] * 7,
+        in_specs=[hbm] * 3 + [vmem] * 3,
         out_specs=vmem,
         scratch_shapes=[
+            pltpu.VMEM(residual.shape, F32),
+            pltpu.VMEM(tangent.shape, F32),
+            pltpu.VMEM(ends.shape, jnp.int32),
+            pltpu.SemaphoreType.DMA((3,)),
             pltpu.VMEM((1, blocks), jnp.int32),
             pltpu.VMEM((blocks, LANES), F32),
             pltpu.VMEM((n, 1, GROUP), F32),
@@ -558,12 +581,12 @@
     )(
         residual,
         tangent,
-        jacobi,
         ends,
-        target.reshape(1, blocks),
+        target.T,
         node_block.reshape(1, blocks),
         cells,
     )
+    return jacobi * residual + lifted
 
 
 def solution(mesh):

time: 75.3 us -> 71 us (0.943)
  the two profiles are of different devices: /device:TPU:16 before, /device:TPU:0 now
where the time goes in v4:
time: 71 us; the launch traced here: 70.8 us
  Pallas kernels  67.6 us (95%)
  local copies, waits for them, and re-layouts  2.13 us (3%)
  other arithmetic  1.02 us (1%)
    pallas_call x1, Pallas kernels, per_device(): pl.pallas_call(functools.partial(kernel, n, n_node, slices), out_shape=ja...  67.6 us

profile of v4, /device:TPU:0, one launch (start us, length us, event | category | flops | bytes accessed | tf_op | source)
XLA Modules:
  0.0 70.8 jit_solution(2594331892375167334)
XLA Ops:
  0.0 1.1 %reshape.7 = f32[4,2,128,32]{3,2,1,0:T(8,128)S(1)} reshape(f32[4,32,256]{2,1,0:T(8,128)} %param.13) | data formatting | bytes 262144 | tf_op jit(solution)/shard_map/reshape | solution.py:531
  1.1 0.0 copy-start.1
  1.1 0.0 copy-start.4
  1.1 0.0 copy-start.2
  1.2 0.0 copy-start
  1.2 0.0 copy-start.3
  1.2 0.3 pad_maximum_fusion.sigma_ref
  1.5 0.8 %copy-done.1 = f32[3,64,1024]{2,1,0:T(8,128)S(1)} copy-done((f32[3,64,1024]{2,1,0:T(8,128)S(1)}, f32[3,64,1024]{2,1,0:T(8,128)}, u32[]{:S(2)}) %copy-start.1) | copy-done | bytes 786456
  2.2 0.0 copy-done.4
  2.2 0.2 copy-done.2
  2.4 0.1 copy-done
  2.4 0.0 copy-done.3
  2.5 0.0 copy-start.5
  2.5 67.6 %shard_map.73 = f32[64,1024]{1,0:T(8,128)S(1)} custom-call(f32[64,1024]{1,0:T(8,128)S(1)} %copy-done, f32[3,64,1024]{2,1,0:T(8,128)S(1)} %copy-done.1, s32[2,64,1024]{2,1,0:T(8,128)S(1)} %copy-done.2, s32[1,1024]{1,0:T(1,128)S(1)} %bitcast.4, s32[1,1024]{1,0:T(1,128)S(1)} %bitcast.5, f32[512,128]{1,0:T(8,128)S(1)} %pad_maximum_fusion.sigma_ref), custom_call_target="tpu_custom_call" | custom-call | tf_op jit(solution)/shard_map/pallas_call | solution.py:537
  70.1 0.0 copy-done.5
  70.1 0.8 %multiply_add_fusion = f32[64,1024]{1,0:T(8,128)} fusion(f32[64,1024]{1,0:T(8,128)S(1)} %shard_map.73, f32[64,1024]{1,0:T(8,128)S(1)} %copy-done.5, f32[64,1024]{1,0:T(8,128)S(1)} %copy-done), kind=kLoop, calls=%fused_computation.1 | loop fusion | flops 131072 | bytes 1048576 | tf_op jit(solution)/shard_map/add | solution.py:589
  (1 shorter events, 0.0 us)
Async XLA Ops:
  1.1 1.1 %copy-start.1 = (f32[3,64,1024]{2,1,0:T(8,128)S(1)}, f32[3,64,1024]{2,1,0:T(8,128)}, u32[]{:S(2)}) copy-start(f32[3,64,1024]{2,1,0:T(8,128)} %tangent_in.1) | copy-start | bytes 2359300
  1.1 1.1 %copy-start.4 = (s32[1024]{0:T(1024)S(1)}, s32[1024]{0:T(1024)}, u32[]{:S(2)}) copy-start(s32[1024]{0:T(1024)} %param.12) | copy-start | bytes 12292
  1.1 1.2 %copy-start.2 = (s32[2,64,1024]{2,1,0:T(8,128)S(1)}, s32[2,64,1024]{2,1,0:T(8,128)}, u32[]{:S(2)}) copy-start(s32[2,64,1024]{2,1,0:T(8,128)} %ends_in.1) | copy-start | bytes 1572868
  1.2 1.3 %copy-start = (f32[64,1024]{1,0:T(8,128)S(1)}, f32[64,1024]{1,0:T(8,128)}, u32[]{:S(2)}) copy-start(f32[64,1024]{1,0:T(8,128)} %resid_in.1) | copy-start | bytes 786436
  1.2 1.3 %copy-start.3 = (s32[1024,1]{0,1:T(1,128)S(1)}, s32[1024,1]{0,1:T(1,128)}, u32[]{:S(2)}) copy-start(s32[1024,1]{0,1:T(1,128)} %param.11) | copy-start | bytes 12292
  2.5 67.6 %copy-start.5 = (f32[64,1024]{1,0:T(8,128)S(1)}, f32[64,1024]{1,0:T(8,128)}, u32[]{:S(2)}) copy-start(f32[64,1024]{1,0:T(8,128)} %param.9) | copy-start | bytes 786436

commit v5 on v4

--- a/solution.py
+++ b/solution.py
@@ -483,7 +483,19 @@
 
         lax.fori_loop(0, lane_groups, lift_group, 0)
 
-    wide_sigma_ref[at_slices(0, slices, 2)] = sigma_ref[...]
+    lane = lax.broadcasted_iota(jnp.int32, (1, LANES), 1)
+    radial = sigma_ref.shape[1] // 2
+    for s in range(slices):
+        for k in range(8):
+            first_lane = k * NODE_BLOCK % LANES
+            at = slice(k * NODE_BLOCK // LANES * LANES, k * NODE_BLOCK // LANES * LANES + LANES)
+            cells = sigma_ref[s, :, at]
+            if first_lane:
+                cells = pltpu.roll(cells, LANES - first_lane, 1)
+            cells = jnp.where(lane < NODE_BLOCK, cells, 0.0)
+            cells = cells + pltpu.roll(cells, NODE_BLOCK, 1)
+            cells = cells[:radial] + pltpu.roll(cells[radial:], LANES // 2, 1)
+            wide_sigma_ref[pl.ds((s + 2) * slab + k, radial, stride=8), :] = cells
     for load in loads:
         load.wait()
     find_terms(0)
@@ -493,19 +505,19 @@
     for side in range(2):
         sigma_halo(side).start()
     find_terms(1)
-    send_terms(1, order[: groups // 2])
+    send_terms(1, order[: groups // 4])
     prepare_return()
     take_labels()
     sum_terms(0)
     for side in range(2):
         halo(0, side).start()
-    send_terms(1, order[groups // 2 :])
+    send_terms(1, order[groups // 4 :])
     smooth(0)
-    send_back(0, order[: groups // 2])
+    send_back(0, order[: groups // 4])
     sum_terms(1)
     for side in range(2):
         halo(1, side).start()
-    send_back(0, order[groups // 2 :])
+    send_back(0, order[groups // 4 :])
     smooth(1)
     send_back(1, order)
     for half in range(2):
@@ -528,12 +540,9 @@
     nodal = slices * rows_radial * rows_axial // NODE_BLOCK // 2
     slots = 2 * blocks
     rows = slots // 2
-    parts = sigma.reshape(slices, 2, LANES, NODE_BLOCK)
-    inner, outer = (parts[:, k].reshape(nodal, NODE_BLOCK) for k in range(2))
-    cells = jnp.concatenate([inner, inner, outer, outer], axis=1)
     groups = slots // GROUP
     vmem = pl.BlockSpec(memory_space=pltpu.VMEM)
-    hbm = pl.BlockSpec(memory_space=pl.ANY)
+    hbm = pl.BlockSpec(memory_space=pltpu.HBM)
     lifted = pl.pallas_call(
         functools.partial(kernel, n, n_node, slices),
         out_shape=jax.ShapeDtypeStruct(residual.shape, F32),
@@ -576,7 +585,7 @@
             pltpu.SemaphoreType.DMA((2,)),
         ],
         compiler_params=pltpu.CompilerParams(
-            collective_id=0, has_side_effects=True, vmem_limit_bytes=48 * 1024 * 1024
+            collective_id=0, has_side_effects=True, vmem_limit_bytes=63 * 1024 * 1024
         ),
     )(
         residual,
@@ -584,7 +593,7 @@
         ends,
         target.T,
         node_block.reshape(1, blocks),
-        cells,
+        sigma,
     )
     return jacobi * residual + lifted
 

time: 71 us -> 73.1 us (1.030)
  Pallas kernels: 67.6 us -> 71.1 us
  local copies, waits for them, and re-layouts: 2.13 us -> 0.01 us
    pallas_call x1, Pallas kernels: 67.6 us -> 71.1 us  [per_device(): pl.pallas_call(functools.partial(kernel, n, n_node, slices), out_shape=ja...]
    reshape x1 -> x0, local copies, waits for them, and re-layouts: 1.07 us -> none  [per_device(): parts = sigma.reshape(slices, 2, LANES, NODE_BLOCK)]
    unnamed x12 -> x4, local copies, waits for them, and re-layouts: 1.02 us -> 0.01 us
    add x1, other arithmetic: 0.75 us -> 1.7 us  [per_device(): return jacobi * residual + lifted]
where the time goes in v5:
time: 73.1 us; the launch traced here: 72.9 us
  Pallas kernels  71.1 us (97%)
  other arithmetic  1.7 us (2%)
    pallas_call x1, Pallas kernels, per_device(): pl.pallas_call(functools.partial(kernel, n, n_node, slices), out_shape=ja...  71.1 us
    add x1, other arithmetic, per_device(): return jacobi * residual + lifted  1.7 us

profile of v5, /device:TPU:0, one launch (start us, length us, event | category | flops | bytes accessed | tf_op | source)
XLA Modules:
  0.0 72.9 jit_solution(12245034749232756525)
XLA Ops:
  0.0 0.0 copy-start
  0.0 0.0 copy-start.1
  0.0 71.1 %shard_map.73 = f32[64,1024]{1,0:T(8,128)} custom-call(f32[64,1024]{1,0:T(8,128)} %resid_in.1, f32[3,64,1024]{2,1,0:T(8,128)} %tangent_in.1, s32[2,64,1024]{2,1,0:T(8,128)} %ends_in.1, s32[1,1024]{1,0:T(1,128)} %bitcast.2, s32[1,1024]{1,0:T(1,128)} %bitcast.3, f32[4,32,256]{2,1,0:T(8,128)} %sigma_ref.1), custom_call_target="tpu_custom_call" | custom-call | tf_op jit(solution)/shard_map/pallas_call | solution.py:546
  71.1 0.0 copy-done
  71.1 0.0 copy-done.1
  71.2 1.7 %multiply_add_fusion = f32[64,1024]{1,0:T(8,128)} fusion(f32[64,1024]{1,0:T(8,128)} %shard_map.73, f32[64,1024]{1,0:T(8,128)S(1)} %copy-done.1, f32[64,1024]{1,0:T(8,128)S(1)} %copy-done), kind=kLoop, calls=%fused_computation | loop fusion | flops 131072 | bytes 1048576 | tf_op jit(solution)/shard_map/add | solution.py:598
Async XLA Ops:
  0.0 71.1 %copy-start = (f32[64,1024]{1,0:T(8,128)S(1)}, f32[64,1024]{1,0:T(8,128)}, u32[]{:S(2)}) copy-start(f32[64,1024]{1,0:T(8,128)} %resid_in.1) | copy-start | bytes 786436
  0.0 71.1 %copy-start.1 = (f32[64,1024]{1,0:T(8,128)S(1)}, f32[64,1024]{1,0:T(8,128)}, u32[]{:S(2)}) copy-start(f32[64,1024]{1,0:T(8,128)} %param.9) | copy-start | bytes 786436
